TPU v7x, 512 devices: a whole 4x4x16 slice. The times are simulated.
512 devices in a mesh: tile: 32 (over x, y, core), slide: 16 (over z).
Axes of the slice: x: 4, y: 4, z: 16, core: 2. Of those that a mesh axis runs over, the one named last changes fastest.
Arguments:
- tile_maps: bfloat16 [8192, 8, 8, 768], P(('tile', 'slide')), may hold values from -6 to 6
- dw_kernel: bfloat16 [49, 768], replicated, may hold values from -0.875 to 0.875
- conv_bias: float32 [768], replicated, may hold values from -0.9 to 0.9
- norm_gain: float32 [768], replicated, may hold values from 0.1 to 1.9
- w_in: bfloat16 [768, 768], replicated, may hold values from -1.75 to 1.75
- w_qkv: bfloat16 [768, 2304], P(None, 'slide'), may hold values from -0.21875 to 0.21875
- seg_len: int32 [16], replicated, may hold values from 4 to 16, as said below
- dilation: int32 [16], replicated, may hold values from 1 to 4, as said below
- tile_slot: int32 [8192], P(('tile', 'slide')), may hold values from 0 to 255, as said below
- slide_lengths: int32 [512, 2], P(('tile', 'slide')), may hold values from 0 to 16, as said below
- cotangent: bfloat16 [8192, 768], P(('tile', 'slide')), may hold values from -0.119628906 to 0.119628906
Outputs:
- attn_out: bfloat16 [8192, 768], P(('tile', 'slide'))
- grad_kernel: float32 [49, 768], replicated
- grad_norm: float32 [2, 768], replicated
Inputs may be any that keep to these rules, and one draw needn't show every extreme that they name: `tile_slot`: within each group, the tiles' slots are each of 0 to 255 once; slot // 16 is the owner along slide; at most 3 tiles of one device go to one owner, and that many do in every draw. `slide_lengths`: each owner's two lengths add up to 16. `seg_len`: each is 4, 8 or 16, and each of the three occurs. `dilation`: each is 1, 2 or 4, and each of the three occurs.
All inputs are finite; a program needn't handle non-finite values.
Results may differ from a plain program's by a relative error of at most 0.024.
Values may be sent and summed in bfloat16 or wider, within the bound.
A program may use at most 64 MiB of HBM per device.

v0:
```python
import jax
import jax.numpy as jnp
from jax import lax
from jax.sharding import PartitionSpec as P

norm_eps = 1e-06


def contract_first(left, right):
    return lax.dot_general(
        left, right, (((0,), (0,)), ((), ())), preferred_element_type=jnp.float32
    )


def contract_last(left, right):
    return lax.dot_general(
        left, right, (((1,), (1,)), ((), ())), preferred_element_type=jnp.float32
    )


def encode(tile_maps, dw_kernel, conv_bias, norm_gain, w_in):
    channels = tile_maps.shape[3]
    conv = (
        lax.conv_general_dilated(
            tile_maps,
            dw_kernel.reshape(7, 7, 1, channels),
            (1, 1),
            ((3, 3), (3, 3)),
            dimension_numbers=("NHWC", "HWIO", "NHWC"),
            feature_group_count=channels,
            preferred_element_type=jnp.float32,
        )
        + conv_bias
    )
    centered = conv - jnp.mean(conv, axis=3, keepdims=True)
    inverse_std = lax.rsqrt(jnp.mean(centered * centered, axis=3, keepdims=True) + norm_eps)
    normed = centered * inverse_std
    pooled = jnp.mean(normed * norm_gain, axis=(1, 2)).astype(jnp.bfloat16)
    embed = jnp.dot(pooled, w_in, preferred_element_type=jnp.float32).astype(jnp.bfloat16)
    return (embed, normed, inverse_std)


def tile_grads(tile_maps, normed, inverse_std, norm_gain, w_in, dembed):
    side = tile_maps.shape[1]
    area = side * side
    dpool = contract_last(dembed, w_in)
    dnormed = dpool[:, None, None, :] * (norm_gain / area)
    inner = jnp.mean(dnormed, axis=3, keepdims=True)
    along = jnp.mean(dnormed * normed, axis=3, keepdims=True)
    dconv = inverse_std * (dnormed - inner - normed * along)
    padded = jnp.pad(tile_maps, ((0, 0), (3, 3), (3, 3), (0, 0)))
    taps = [
        jnp.sum(
            padded[:, row_off : row_off + side, col_off : col_off + side, :].astype(jnp.float32)
            * dconv,
            axis=(0, 1, 2),
        )
        for row_off in range(7)
        for col_off in range(7)
    ]
    grad_bias = jnp.sum(dconv, axis=(0, 1, 2))
    grad_gain = jnp.sum(dpool * jnp.sum(normed, axis=(1, 2)), axis=0) / area
    return (jnp.stack(taps), jnp.stack([grad_bias, grad_gain]))


def slot_layout(lengths, capacity):
    owners, slides = lengths.shape
    ends = jnp.cumsum(lengths, axis=1)
    index = jnp.arange(capacity, dtype=jnp.int32)
    label = jnp.sum((index[None, :, None] >= ends[:, None, :]).astype(jnp.int32), axis=2)
    match = label[:, :, None] == jnp.arange(slides, dtype=jnp.int32)[None, None, :]
    begin = jnp.sum(jnp.where(match, (ends - lengths)[:, None, :], 0), axis=2)
    position = index[None, :] - begin
    slide_id = jnp.arange(owners, dtype=jnp.int32)[:, None] * slides + label
    return (slide_id.reshape(-1), position.reshape(-1))


def head_mask(slide_id, position, seg_len, dilation):
    same = slide_id[:, None] == slide_id[None, :]
    segment = position[None, :] // seg_len[:, None]
    residue = position[None, :] % dilation[:, None]
    return (
        same[None]
        & (segment[:, :, None] == segment[:, None, :])
        & (residue[:, :, None] == residue[:, None, :])
    )


def head_pass(qkv, upstream, allowed, scale):
    queries = qkv[:, :, 0]
    key_rows = qkv[:, :, 1]
    value_rows = qkv[:, :, 2]
    scores = (
        jnp.einsum("ihd,jhd->hij", queries, key_rows, preferred_element_type=jnp.float32) * scale
    )
    masked = jnp.where(allowed, scores, -1e30)
    top = jnp.max(masked, axis=2, keepdims=True)
    expo = jnp.where(allowed, jnp.exp(masked - top), 0.0)
    prob = expo / jnp.sum(expo, axis=2, keepdims=True)
    weights = prob.astype(jnp.bfloat16)
    mixed = jnp.einsum(
        "hij,jhd->ihd", weights, value_rows, preferred_element_type=jnp.float32
    ).astype(jnp.bfloat16)
    dprob = jnp.einsum("ihd,jhd->hij", upstream, value_rows, preferred_element_type=jnp.float32)
    dvalue = jnp.einsum("hij,ihd->jhd", weights, upstream, preferred_element_type=jnp.float32)
    dscore = (prob * (dprob - jnp.sum(prob * dprob, axis=2, keepdims=True)) * scale).astype(
        jnp.bfloat16
    )
    dquery = jnp.einsum("hij,jhd->ihd", dscore, key_rows, preferred_element_type=jnp.float32)
    dkey = jnp.einsum("hij,ihd->jhd", dscore, queries, preferred_element_type=jnp.float32)
    dqkv = jnp.stack([dquery, dkey, dvalue], axis=2).astype(jnp.bfloat16)
    return (mixed, dqkv)


def body(
    tile_maps,
    dw_kernel,
    conv_bias,
    norm_gain,
    w_in,
    w_qkv,
    seg_len,
    dilation,
    tile_slot,
    slide_lengths,
    cotangent,
):
    count = tile_maps.shape[0]
    width = w_in.shape[1]
    heads = seg_len.shape[0]
    head_size = width // heads
    scale = head_size ** (-0.5)
    devices = lax.axis_size("slide")
    owner_self = lax.axis_index("slide")
    embed, normed, inverse_std = encode(tile_maps, dw_kernel, conv_bias, norm_gain, w_in)
    quota = max(2, (3 * count + devices - 1) // devices)
    owner = tile_slot // count
    order = jnp.arange(count, dtype=jnp.int32)
    earlier = (owner[:, None] == owner[None, :]) & (order[None, :] < order[:, None])
    rank = jnp.sum(earlier.astype(jnp.int32), axis=1)
    target = owner * quota + rank
    select = target[:, None] == jnp.arange(devices * quota, dtype=jnp.int32)[None, :]
    select_bf = select.astype(jnp.bfloat16)
    outgoing = contract_first(select_bf, embed).astype(jnp.bfloat16)
    carried = (
        jnp.sum(jnp.where(select, tile_slot[:, None], 0), axis=0)
        + jnp.sum(select.astype(jnp.int32), axis=0)
        - 1
    )
    arrived, arrived_slot = (
        lax.all_to_all(
            outgoing.reshape(devices, quota, width),
            "slide",
            split_axis=0,
            concat_axis=0,
            tiled=True,
        ),
        lax.all_to_all(
            carried.reshape(devices, quota), "slide", split_axis=0, concat_axis=0, tiled=True
        ),
    )
    local = arrived_slot.reshape(-1) - owner_self * count
    place = (local[:, None] == jnp.arange(count, dtype=jnp.int32)[None, :]).astype(jnp.bfloat16)
    block = contract_first(place, arrived.reshape(-1, width)).astype(jnp.bfloat16)
    full = lax.all_gather(w_qkv, "slide", axis=1, tiled=True)
    slide_id, position = slot_layout(slide_lengths, count)
    allowed = head_mask(slide_id, position, seg_len, dilation)
    qkv = (
        jnp.dot(block, full, preferred_element_type=jnp.float32)
        .astype(jnp.bfloat16)
        .reshape(count, heads, 3, head_size)
    )
    mixed, dqkv = head_pass(qkv, cotangent.reshape(count, heads, head_size), allowed, scale)
    attn_out = mixed.reshape(count, width)
    grouped = jnp.einsum(
        "rgk,dgk->grd",
        dqkv.reshape(count, devices, -1),
        full.reshape(width, devices, -1),
        preferred_element_type=jnp.float32,
    )
    dblock = jnp.sum(grouped.astype(jnp.bfloat16).astype(jnp.float32), axis=0).astype(jnp.bfloat16)
    returning = jnp.dot(place, dblock, preferred_element_type=jnp.float32).astype(jnp.bfloat16)
    returned = lax.all_to_all(
        returning.reshape(devices, quota, width), "slide", split_axis=0, concat_axis=0, tiled=True
    )
    dembed = jnp.dot(
        select_bf, returned.reshape(-1, width), preferred_element_type=jnp.float32
    ).astype(jnp.bfloat16)
    kernel_part, norm_part = tile_grads(tile_maps, normed, inverse_std, norm_gain, w_in, dembed)
    grad_kernel, grad_norm = lax.psum((kernel_part, norm_part), ("tile", "slide"))
    return (attn_out, grad_kernel, grad_norm)


def solution(mesh):
    in_specs = (
        P(("tile", "slide"), None, None, None),
        P(),
        P(),
        P(),
        P(),
        P(None, "slide"),
        P(),
        P(),
        P(("tile", "slide")),
        P(("tile", "slide"), None),
        P(("tile", "slide"), None),
    )
    out_specs = (P(("tile", "slide"), None), P(), P())
    return jax.shard_map(body, mesh=mesh, in_specs=in_specs, out_specs=out_specs, check_vma=False)
```

profile of v0, /device:TPU:1, one launch (start us, length us, event | category | flops | bytes accessed | tf_op | source)
XLA Modules:
  0.0 615.0 jit_solution(15794409407857104796)
XLA Ops:
  7.2 0.7 all-gather.2.cloned.1.call-update
  7.9 0.7 and_select_fusion
  8.8 0.7 multiply_add_fusion
  9.4 0.7 convert_reduce_fusion
  10.2 0.7 sub.86
  10.9 15.7 %all-to-all-start = ((s32[16,1,3]{2,1,0:T(1,128)}), s32[16,1,3]{2,1,0:T(1,128)S(1)}, u32[]{:S(2)}, u32[]{:S(2)}) async-start(s32[16,1,3]{2,1,0:T(1,128)} %bitcast), calls=%async_computation | async-start | bytes 16384 | tf_op jit(solution)/shard_map/all_to_all | solution.py:158
  26.6 1.0 reshape.543
  27.7 0.7 sign.22
  28.3 0.8 reduce_window_sum.11
  30.0 0.7 broadcast_compare_fusion.1
  31.3 12.6 %add_reduce_fusion = (f32[16,8,8]{0,2,1:T(8,128)S(1)}, f32[16,8,8,768]{3,0,2,1:T(8,128)S(1)}) fusion(f32[768]{0:T(1024)} %param.13, bf16[7,7,1,768]{3,2,1,0:T(2,128)(2,1)S(1)} %reshape.543, bf16[16,8,8,768]{3,2,1,0:T(8,128)(2,1)} %param.11), kind=kOutput, calls=%fused_computation.105 | convolution fusion | flops 49150976 | bytes 4801024 | tf_op jit(solution)/shard_map/conv_general_dilated | solution.py:24
  44.6 1.0 copy-done.2
  46.9 0.7 reshape.535
  47.7 11.4 %all-to-all-start.1 = ((bf16[16,3,768]{2,1,0:T(4,128)(2,1)}), bf16[16,3,768]{2,1,0:T(4,128)(2,1)S(1)}, u32[]{:S(2)}, u32[]{:S(2)}) async-start(bf16[16,3,768]{2,1,0:T(4,128)(2,1)} %reshape.535), calls=%async_computation.1 | async-start | bytes 196608 | tf_op jit(solution)/shard_map/all_to_all | solution.py:151
  59.4 11.9 %all-to-all-done.1 = bf16[16,3,768]{2,1,0:T(4,128)(2,1)S(1)} async-done(((bf16[16,3,768]{2,1,0:T(4,128)(2,1)}), bf16[16,3,768]{2,1,0:T(4,128)(2,1)S(1)}, u32[]{:S(2)}, u32[]{:S(2)}) %all-to-all-start.1) | async-done | bytes 73760 | tf_op jit(solution)/shard_map/all_to_all | solution.py:151
  71.4 16.2 %all-gather.2.cloned.1.call-done = bf16[768,2304]{0,1:T(8,128)(2,1)} async-done(((bf16[768,144]{0,1:T(8,128)(2,1)}), bf16[768,2304]{0,1:T(8,128)(2,1)}) %all-gather.2.cloned.1.call-update) | async-done | bytes 3538960 | tf_op jit(solution)/shard_map/all_gather | solution.py:165
  87.6 3.2 convolution_convert_fusion
  93.0 2.6 fusion.3
  95.8 0.7 reshape.541
  96.4 6.8 %all-to-all-start.2 = ((bf16[16,3,768]{2,1,0:T(4,128)(2,1)}), bf16[16,3,768]{2,1,0:T(4,128)(2,1)S(1)}, u32[]{:S(2)}, u32[]{:S(2)}) async-start(bf16[16,3,768]{2,1,0:T(4,128)(2,1)} %reshape.541), calls=%async_computation.2 | async-start | bytes 196608 | tf_op jit(solution)/shard_map/all_to_all | solution.py:183
  103.5 2.0 copy.54
  105.8 0.7 reshape.538
  106.5 8.6 %all-to-all-done.2 = bf16[16,3,768]{2,1,0:T(4,128)(2,1)S(1)} async-done(((bf16[16,3,768]{2,1,0:T(4,128)(2,1)}), bf16[16,3,768]{2,1,0:T(4,128)(2,1)S(1)}, u32[]{:S(2)}, u32[]{:S(2)}) %all-to-all-start.2) | async-done | bytes 73760 | tf_op jit(solution)/shard_map/all_to_all | solution.py:183
  115.2 0.7 fusion.51
  115.9 2.9 fusion.2
  118.9 11.5 %multiply_reduce_fusion = (f32[768]{0:T(1024)S(1)}, f32[768]{0:T(1024)S(1)}, f32[768]{0:T(1024)S(1)}, f32[768]{0:T(1024)S(1)}, f32[768]{0:T(1024)S(1)}, /*index=...) fusion(bf16[16,8,8,768]{3,0,2,1:T(8,128)(2,1)} %copy.54, ...), kind=kLoop, calls=%fused_computation.51 | loop fusion | flops 47172096 | bytes 7984128 | tf_op jit(solution)/shard_map/reduce_sum | solution.py:53
  130.4 7.2 %fusion.50 = (f32[768]{0:T(1024)S(1)}, f32[768]{0:T(1024)S(1)}, f32[768]{0:T(1024)S(1)}, f32[768]{0:T(1024)S(1)}, f32[768]{0:T(1024)S(1)}, /*index=5*/f32[768]{0...) fusion(f32[16,8,8,768]{3,0,2,1:T(8,128)S(1)} %get-tuple-element, ...), kind=kLoop, calls=%fused_computation.204 | loop fusion | flops 31446528 | bytes 6334464 | tf_op jit(solution)/shard_map/reduce_sum | solution.py:61
  137.6 9.2 %multiply_reduce_fusion.18 = (f32[768]{0:T(1024)S(1)}, f32[768]{0:T(1024)S(1)}, f32[768]{0:T(1024)S(1)}, f32[768]{0:T(1024)S(1)}, f32[768]{0:T(1024)S(1)}, /*ind...) fusion(f32[16,8,8,768]{3,0,2,1:T(8,128)S(1)} %get-tuple-element, ...), kind=kLoop, calls=%fused_computation.69 | loop fusion | flops 42453504 | bytes 4773888 | tf_op jit(solution)/shard_map/reduce_sum | solution.py:53
  147.4 4.5 stack.226
  152.0 110.7 %psum.15 = f32[2,768]{1,0:T(2,128)} all-reduce(f32[2,768]{1,0:T(2,128)S(1)} %pad_maximum_fusion.1), channel_id=1, replica_groups=mesh['tile'=32,'slide'=16] {'tile','slide'}, use_global_device_ids=true, to_apply=%region_68.69 | all-reduce | flops 1536 | bytes 12288 | tf_op jit(solution)/shard_map/psum | solution.py:190
  262.6 343.9 %all-reduce.3.cloned.1.call-done = f32[49,768]{1,0:T(8,128)} async-done(((f32[49,768]{1,0:T(8,128)}), f32[49,768]{1,0:T(8,128)}) %all-reduce.3.cloned.1.call-update) | async-done | bytes 150544 | tf_op jit(solution)/shard_map/psum | solution.py:190
  606.6 1.6 copy.98
  (110 shorter events, 7.1 us)
Async XLA Ops:
  7.2 39.0 %copy-start = (bf16[768,768]{1,0:T(8,128)(2,1)S(1)}, bf16[768,768]{1,0:T(8,128)(2,1)}, u32[]{:S(2)}) copy-start(bf16[768,768]{1,0:T(8,128)(2,1)} %param.15) | copy-start | bytes 3538948
  7.2 80.4 %all-gather.2.cloned.1.call-start = ((), (), s32[]{:S(2)}) async-start(), calls=%async_computation.3 | async-start | bytes 3760128 | tf_op jit(solution)/shard_map/all_gather | solution.py:165
  10.9 36.9 %all-to-all-start = ((s32[16,1,3]{2,1,0:T(1,128)}), s32[16,1,3]{2,1,0:T(1,128)S(1)}, u32[]{:S(2)}, u32[]{:S(2)}) async-start(s32[16,1,3]{2,1,0:T(1,128)} %bitcast), calls=%async_computation | async-start | bytes 16384 | tf_op jit(solution)/shard_map/all_to_all | solution.py:158
  31.3 12.6 %copy-start.5 = (f32[768]{0:T(1024)S(1)}, f32[768]{0:T(1024)}, u32[]{:S(2)}) copy-start(f32[768]{0:T(1024)} %param.13) | copy-start | bytes 9220
  43.9 1.7 copy-start.2
  43.9 1.7 copy-start.7
  44.0 2.6 copy-start.8
  44.5 3.1 copy-start.6
  47.7 23.6 %all-to-all-start.1 = ((bf16[16,3,768]{2,1,0:T(4,128)(2,1)}), bf16[16,3,768]{2,1,0:T(4,128)(2,1)S(1)}, u32[]{:S(2)}, u32[]{:S(2)}) async-start(bf16[16,3,768]{2,1,0:T(4,128)(2,1)} %reshape.535), calls=%async_computation.1 | async-start | bytes 196608 | tf_op jit(solution)/shard_map/all_to_all | solution.py:151
  92.4 11.1 %copy-start.1 = (bf16[16,8,8,768]{3,2,1,0:T(8,128)(2,1)S(1)}, bf16[16,8,8,768]{3,2,1,0:T(8,128)(2,1)}, u32[]{:S(2)}) copy-start(bf16[16,8,8,768]{3,2,1,0:T(8,128)(2,1)} %param.11) | copy-start | bytes 4718596
  96.4 18.7 %all-to-all-start.2 = ((bf16[16,3,768]{2,1,0:T(4,128)(2,1)}), bf16[16,3,768]{2,1,0:T(4,128)(2,1)S(1)}, u32[]{:S(2)}, u32[]{:S(2)}) async-start(bf16[16,3,768]{2,1,0:T(4,128)(2,1)} %reshape.541), calls=%async_computation.2 | async-start | bytes 196608 | tf_op jit(solution)/shard_map/all_to_all | solution.py:183
  103.3 503.3 %all-reduce.3.cloned.1.call-start = ((), (), s32[]{:S(2)}) async-start(), calls=%async_computation.4 | async-start | bytes 344064 | tf_op jit(solution)/shard_map/psum | solution.py:190
  115.9 3.0 copy-start.3
  118.9 11.5 %copy-start.4 = (bf16[16,8,8,768]{3,0,2,1:T(8,128)(2,1)S(1)}, bf16[16,8,8,768]{3,0,2,1:T(8,128)(2,1)}, u32[]{:S(2)}) copy-start(bf16[16,8,8,768]{3,0,2,1:T(8,128)(2,1)} %copy.54) | copy-start | bytes 4718596
Sparse Core Ops, SparseCore 0:
  10.1 77.4 all-gather.1
  152.1 454.4 all-reduce.2
where the time goes:
time: 616 us; the launch traced here: 615 us
  waiting for transfers between devices  381 us (62%)
  blocking collectives  111 us (18%)
  other arithmetic  38.4 us (6%)
  starting transfers between devices  34.3 us (6%)
  matrix products  20.9 us (3%)
  between operations  14.8 us (2%)
  local copies, waits for them, and re-layouts  14.6 us (2%)
    psum x1, waiting for transfers between devices, body(): lax.psum((kernel_part, norm_part), ('tile', 'slide'))  344 us
    psum x1, blocking collectives, body(): lax.psum((kernel_part, norm_part), ('tile', 'slide'))  111 us
    reduce_sum x2, other arithmetic, tile_grads(): jnp.sum(padded[:, row_off:row_off + side, col_off:col_off + side, :].asty...  20.7 us
    all_gather x1, waiting for transfers between devices, body(): full = lax.all_gather(w_qkv, 'slide', axis=1, tiled=True)  16.2 us
    all_to_all x1, starting transfers between devices, body(): lax.all_to_all(carried.reshape(devices, quota), 'slide', split_axis=0, co...  15.7 us
    conv_general_dilated x1, matrix products, encode(): lax.conv_general_dilated(tile_maps, dw_kernel.reshape(7, 7, 1, channels),...  12.6 us
  transfers between devices with their start and end apart: 5, of which 4 were waited for; matrix products, arithmetic and copies ran while one was open for 4% of the time, Pallas kernels for 0%

commit v1 on v0

v1 whole, which is shorter than its diff:
```python
import jax
import jax.numpy as jnp
from jax import lax
from jax.experimental import pallas as pl
from jax.experimental.pallas import tpu as pltpu
from jax.sharding import PartitionSpec as P

NORM_EPS = 1e-06
MESH = pl.DeviceIdType.MESH
BF = jnp.bfloat16
F32 = jnp.float32

SIDE = 8
AREA = SIDE * SIDE
REACH = 3
TAPS = 7
ROWS = 16
C = 768
LANE = 128
CHUNKS = C // LANE
HEADS = 16
HEAD = 48
SLIDES = 16
PLANE = 32
QUOTA = 3
PACK = 32
HALF = C // 2
UNITS = 24
SUM_ROWS = 64


def iota(shape, dim):
    return lax.broadcasted_iota(jnp.int32, shape, dim)


def dot(left, right):
    return jnp.dot(left, right, preferred_element_type=F32)


def dot_last(left, right):
    return lax.dot_general(left, right, (((1,), (1,)), ((), ())), preferred_element_type=F32)


def dot_first(left, right):
    return lax.dot_general(left, right, (((0,), (0,)), ((), ())), preferred_element_type=F32)


def spread(block):
    return jnp.concatenate([block[:, k * LANE : (k + 1) * LANE] for k in range(CHUNKS)], axis=0)


def gather_chunks(stack):
    return jnp.concatenate([stack[k * ROWS : (k + 1) * ROWS] for k in range(CHUNKS)], axis=1)


def row_span(offset):
    return max(0, -offset), min(SIDE, SIDE - offset)


def transpose_maps(maps_ref, xt_ref):
    row, col = iota((128, 128), 0), iota((128, 128), 1)
    perm = ((row >> 4) == (col & 7)) & ((row & 15) == (col >> 3))
    perm = perm.astype(F32).astype(BF)
    for r in range(SIDE):
        part = maps_ref[:, r].astype(F32).reshape(128, C).astype(BF)
        xt_ref[r] = dot(perm, part).astype(BF).reshape(SIDE, ROWS, C)


def spread_taps(dw_ref, wb_ref):
    taps = dw_ref[...].astype(F32)
    for tap in range(TAPS * TAPS):
        wb_ref[tap] = jnp.broadcast_to(taps[tap : tap + 1], (ROWS, C)).astype(BF)


def conv_chunk(chunk, xt_ref, wb_ref, bias_ref, cv_ref):
    lanes = pl.ds(pl.multiple_of(chunk * LANE, LANE), LANE)
    bias = jnp.broadcast_to(bias_ref[:, lanes], (ROWS, LANE))
    for i in range(SIDE):
        total = [bias] * SIDE
        for r in range(TAPS):
            src = i + r - REACH
            if not 0 <= src < SIDE:
                continue
            cells = [xt_ref[src, j, :, lanes] for j in range(SIDE)]
            taps = [wb_ref[r * TAPS + s, :, lanes] for s in range(TAPS)]
            for j in range(SIDE):
                acc = None
                for s in range(TAPS):
                    at = j + s - REACH
                    if 0 <= at < SIDE:
                        term = cells[at] * taps[s]
                        acc = term if acc is None else acc + term
                total[j] = total[j] + acc.astype(F32)
        for j in range(SIDE):
            cv_ref[i * SIDE + j, :, lanes] = total[j]


def normalise(cv_ref, nrm_ref, inv_ref):
    def step(p, total):
        conv = cv_ref[p]
        centered = conv - jnp.mean(conv, axis=1, keepdims=True)
        inv = lax.rsqrt(jnp.mean(centered * centered, axis=1, keepdims=True) + NORM_EPS)
        normed = centered * inv
        nrm_ref[p] = normed.astype(BF)
        inv_ref[p] = jnp.broadcast_to(inv, (ROWS, LANE))
        return total + normed

    return lax.fori_loop(0, AREA, step, jnp.zeros((ROWS, C), F32), unroll=2)


def forward_kernel(
    maps_ref, dw_ref, bias_ref, gain_ref, win_ref,
    xt_ref, nrm_ref, inv_ref, sum_ref, embed_ref,
    wb_ref, cv_ref,
):
    transpose_maps(maps_ref, xt_ref)
    spread_taps(dw_ref, wb_ref)

    @pl.loop(0, CHUNKS)
    def _(chunk):
        conv_chunk(chunk, xt_ref, wb_ref, bias_ref, cv_ref)

    total = normalise(cv_ref, nrm_ref, inv_ref)
    sum_ref[...] = total
    pooled = (total * gain_ref[...] * (1.0 / AREA)).astype(BF)
    embed_ref[...] = dot(pooled, win_ref[...]).astype(BF)


def send_rows(slot_ref):
    lane = iota((1, 112), 1)
    tile, chunk = lane & 15, lane >> 4
    owner = jnp.zeros((1, 112), jnp.int32)
    for t in range(ROWS):
        owner = jnp.where(tile == t, slot_ref[t] >> 4, owner)
    rank = jnp.zeros((1, 112), jnp.int32)
    for t in range(ROWS):
        rank = rank + jnp.where((owner == (slot_ref[t] >> 4)) & (tile > t), 1, 0)
    want = owner * PACK + chunk * QUOTA + rank
    select = (iota((SLIDES * PACK, 112), 0) == want).astype(F32).astype(BF)
    sub = iota((ROWS, LANE), 0)
    slots = jnp.zeros((ROWS, LANE), jnp.int32)
    for t in range(ROWS):
        slots = jnp.where(sub == t, (slot_ref[t] & 15) + 1, slots)
    return select, slots.astype(F32).astype(BF)


def slot_spread():
    size = SLIDES * PACK
    row, col = iota((size, size), 0), iota((size, size), 1)
    inside = row & (PACK - 1)
    quota = inside
    for k in range(1, PACK // QUOTA + 1):
        quota = jnp.where(inside >= k * QUOTA, inside - k * QUOTA, quota)
    return (col == (row - inside + CHUNKS * QUOTA + quota)).astype(F32).astype(BF)


def place_rows(spread_slots, arrived):
    size = SLIDES * PACK
    slot = dot(spread_slots, arrived)[:, : CHUNKS * ROWS]
    inside = iota((size, CHUNKS * ROWS), 0) & (PACK - 1)
    lane = iota((size, CHUNKS * ROWS), 1)
    first = (lane >> 4) * QUOTA
    want = ((lane & 15) + 1).astype(F32)
    hit = (inside >= first) & (inside < first + QUOTA) & (slot == want)
    return hit.astype(F32).astype(BF)


def head_mask():
    row, lane = iota((HEADS * ROWS, C), 0), iota((HEADS * ROWS, C), 1)
    low = (row >> 4) * HEAD
    return ((lane >= low) & (lane < low + HEAD)).astype(F32).astype(BF)


def allowed_pairs(seg_ref, dil_ref, len_ref):
    left, right = iota((ROWS, ROWS), 0), iota((ROWS, ROWS), 1)
    cut = len_ref[0, 0]
    run_left, run_right = left >= cut, right >= cut
    pos_left = jnp.where(run_left, left - cut, left)
    pos_right = jnp.where(run_right, right - cut, right)
    apart = pos_left ^ pos_right
    apart = jnp.where(run_left != run_right, apart | 256, apart)
    parts = []
    for h in range(HEADS):
        parts.append(apart & (~(seg_ref[h] - 1) | (dil_ref[h] - 1)))
    return jnp.concatenate(parts, axis=0) == 0


def attention(block, w3_ref, cot_ref, attn_ref, mask, allowed):
    scale = HEAD ** (-0.5)
    weights = [w3_ref[part].reshape(C, C) for part in range(3)]
    query, key, value = [dot_last(block, each).astype(BF) for each in weights]
    many_query = jnp.concatenate([query] * HEADS, axis=0) * mask
    many_grad = jnp.concatenate([cot_ref[...]] * HEADS, axis=0) * mask
    scores = dot_last(many_query, key) * scale
    masked = jnp.where(allowed, scores, -1e30)
    top = jnp.max(masked, axis=1, keepdims=True)
    expo = jnp.where(allowed, jnp.exp(masked - top), 0.0)
    prob = expo / jnp.sum(expo, axis=1, keepdims=True)
    prob_bf = prob.astype(BF)
    mask_f = mask.astype(F32)

    def own_head(full):
        return jnp.sum((full * mask_f).reshape(HEADS, ROWS, C), axis=0)

    attn_ref[...] = own_head(dot(prob_bf, value)).astype(BF)
    dprob = dot_last(many_grad, value)
    dscore = (prob * (dprob - jnp.sum(prob * dprob, axis=1, keepdims=True)) * scale).astype(BF)
    dquery = own_head(dot(dscore, key)).astype(BF)
    dkey = dot_first(dscore, many_query).astype(BF)
    dvalue = dot_first(prob_bf, many_grad).astype(BF)
    total = dot(dquery, weights[0]) + dot(dkey, weights[1]) + dot(dvalue, weights[2])
    return total.astype(BF)


def shift(index, by, size):
    return lax.rem(index + by + size, size)


def core_of(tile):
    return lax.rem(tile, 2)


class Ring:
    def __init__(self, w3_ref, sems):
        self.w3_ref = w3_ref
        self.right, self.left, self.core = sems[0:2], sems[2:4], sems[4:6]
        tile = lax.axis_index("tile")
        self.me = lax.axis_index("slide")
        self.lanes = pl.ds(pl.multiple_of(core_of(tile) * HALF, HALF), HALF)
        self.other = tile + 1 - 2 * core_of(tile)

    def copy(self, head, send_sem, recv_sem, device):
        block = self.w3_ref.at[:, head, :, self.lanes]
        return pltpu.make_async_remote_copy(
            block, block, send_sem, recv_sem, device_id=device, device_id_type=MESH)

    def to_right(self, s):
        return self.copy(
            shift(self.me, -s, SLIDES), self.right[0].at[s], self.right[1].at[s],
            {"slide": shift(self.me, 1, SLIDES)})

    def to_left(self, s):
        return self.copy(
            shift(self.me, s, SLIDES), self.left[0].at[s], self.left[1].at[s],
            {"slide": shift(self.me, -1, SLIDES)})

    def left_to_core(self, s):
        return self.copy(
            shift(self.me, -s, SLIDES), self.core[0].at[0, s], self.core[1].at[0, s],
            {"tile": self.other})

    def right_to_core(self, s):
        return self.copy(
            shift(self.me, s, SLIDES), self.core[0].at[1, s], self.core[1].at[1, s],
            {"tile": self.other})


RIGHT_STEPS = SLIDES // 2
LEFT_STEPS = SLIDES // 2 - 1


def ring_start(wq_ref, w3_ref, ring):
    w3_ref[:, ring.me] = wq_ref[...].reshape(3, HEAD, C)
    ring.to_right(0).start()
    ring.to_left(0).start()


def ring_step(ring, s):
    ring.to_right(s - 1).wait_recv()
    if s < RIGHT_STEPS:
        ring.to_right(s).start()
    ring.left_to_core(s).start()
    if s <= LEFT_STEPS:
        ring.to_left(s - 1).wait_recv()
        if s < LEFT_STEPS:
            ring.to_left(s).start()
        ring.right_to_core(s).start()


def ring_end(ring):
    for s in range(RIGHT_STEPS + 1):
        if s >= 1:
            ring.left_to_core(s).wait()
        if 1 <= s <= LEFT_STEPS:
            ring.right_to_core(s).wait()
        if s < RIGHT_STEPS:
            ring.to_right(s).wait_send()
        if s < LEFT_STEPS:
            ring.to_left(s).wait_send()


def exchange_start(out_ref, in_ref, send_sem, recv_sem):
    me = lax.axis_index("slide")
    in_ref[me] = out_ref[me]

    @pl.loop(1, SLIDES)
    def _(j):
        peer = shift(me, j, SLIDES)
        pltpu.make_async_remote_copy(
            out_ref.at[peer], in_ref.at[me], send_sem, recv_sem,
            device_id={"slide": peer}, device_id_type=MESH).start()


def exchange_wait(out_ref, in_ref, send_sem, recv_sem):
    some = pl.ds(0, SLIDES - 1)
    pltpu.make_async_copy(in_ref.at[some], in_ref.at[some], recv_sem).wait()
    pltpu.make_async_copy(out_ref.at[some], out_ref.at[some], send_sem).wait()


def greet(with_plane):
    tile, me = lax.axis_index("tile"), lax.axis_index("slide")
    barrier = pltpu.get_barrier_semaphore()

    @pl.loop(1, SLIDES)
    def _(j):
        pl.semaphore_signal(
            barrier, inc=1, device_id={"slide": shift(me, j, SLIDES)}, device_id_type=MESH)

    count = SLIDES - 1
    if with_plane:

        @pl.loop(1, PLANE)
        def _(j):
            pl.semaphore_signal(
                barrier, inc=1, device_id={"tile": shift(tile, j, PLANE)}, device_id_type=MESH)

        count += PLANE - 1
    else:
        pl.semaphore_signal(
            barrier, inc=1, device_id={"tile": tile + 1 - 2 * core_of(tile)}, device_id_type=MESH)
        count += 1
    pl.semaphore_wait(barrier, count)


def owner_kernel(
    embed_ref, win_ref, wq_ref, seg_ref, dil_ref, slot_ref, len_ref, cot_ref,
    attn_ref, dpool_ref,
    w3_ref, out_ref, in_ref, back_out_ref, back_in_ref,
    right_send, right_recv, left_send, left_recv, core_send, core_recv, route_sems,
):
    sems = (right_send, right_recv, left_send, left_recv, core_send, core_recv)
    greet(False)
    ring = Ring(w3_ref, sems)
    ring_start(wq_ref, w3_ref, ring)
    select, slots = send_rows(slot_ref)
    packed = jnp.concatenate([spread(embed_ref[...]), slots], axis=0)
    out_ref[...] = dot(select, packed).astype(BF).reshape(SLIDES, PACK, LANE)
    exchange_start(out_ref, in_ref, route_sems.at[0], route_sems.at[1])
    spread_slots, mask = slot_spread(), head_mask()
    allowed = allowed_pairs(seg_ref, dil_ref, len_ref)
    for s in range(1, RIGHT_STEPS + 1):
        ring_step(ring, s)
    exchange_wait(out_ref, in_ref, route_sems.at[0], route_sems.at[1])
    arrived = in_ref[...].reshape(SLIDES * PACK, LANE)
    place = place_rows(spread_slots, arrived)
    block = gather_chunks(dot_first(place, arrived).astype(BF))
    ring_end(ring)
    dblock = attention(block, w3_ref, cot_ref, attn_ref, mask, allowed)
    back_out_ref[...] = dot(place, spread(dblock)).astype(BF).reshape(SLIDES, PACK, LANE)
    exchange_start(back_out_ref, back_in_ref, route_sems.at[2], route_sems.at[3])
    exchange_wait(back_out_ref, back_in_ref, route_sems.at[2], route_sems.at[3])
    returned = back_in_ref[...].reshape(SLIDES * PACK, LANE)
    dembed = gather_chunks(dot_first(select[:, : CHUNKS * ROWS], returned).astype(BF))
    dpool_ref[...] = dot_last(dembed, win_ref[...])


def conv_grads(dpool, gain_ref, nrm_ref, inv_ref, dc_ref):
    grad = dpool * (gain_ref[...] * (1.0 / AREA))
    level = grad - jnp.mean(grad, axis=1, keepdims=True)

    def step(p, total):
        normed = nrm_ref[p].astype(F32)
        along = jnp.mean(grad * normed, axis=1, keepdims=True)
        inv = inv_ref[p][:, :1]
        dconv = inv * (level - normed * along)
        dc_ref[p] = dconv.astype(BF)
        return total + dconv

    return lax.fori_loop(0, AREA, step, jnp.zeros((ROWS, C), F32), unroll=2)


def tap_grads(chunk, xt_ref, dc_ref, part_ref):
    lanes = pl.ds(pl.multiple_of(chunk * LANE, LANE), LANE)
    for r in range(TAPS):
        total = [jnp.zeros((ROWS, LANE), F32)] * TAPS
        for i in range(*row_span(r - REACH)):
            cells = [xt_ref[i + r - REACH, j, :, lanes] for j in range(SIDE)]
            grads = [dc_ref[i * SIDE + j, :, lanes] for j in range(SIDE)]
            for s in range(TAPS):
                acc = None
                for j in range(*row_span(s - REACH)):
                    term = cells[j + s - REACH] * grads[j]
                    acc = term if acc is None else acc + term
                total[s] = total[s] + acc.astype(F32)
        for s in range(TAPS):
            tap = r * TAPS + s
            part_ref[tap : tap + 1, lanes] = jnp.sum(total[s], axis=0, keepdims=True)


def backward_kernel(dpool_ref, gain_ref, xt_ref, nrm_ref, inv_ref, sum_ref, part_ref, dc_ref):
    dpool = dpool_ref[...]
    bias_grad = conv_grads(dpool, gain_ref, nrm_ref, inv_ref, dc_ref)
    part_ref[...] = jnp.zeros(part_ref.shape, F32)
    part_ref[49:50] = jnp.sum(bias_grad, axis=0, keepdims=True)
    part_ref[50:51] = jnp.sum(dpool * sum_ref[...], axis=0, keepdims=True) * (1.0 / AREA)

    @pl.loop(0, CHUNKS)
    def _(chunk):
        tap_grads(chunk, xt_ref, dc_ref, part_ref)


def unit_at(ref, unit):
    rows = pl.ds(pl.multiple_of((unit & 3) * 16, 16), 16)
    lanes = pl.ds(pl.multiple_of((unit >> 2) * LANE, LANE), LANE)
    return ref.at[rows, lanes]


def owner_of(unit):
    return unit + unit // 3


def reduce_all(flat_ref, near_ref, far_ref, res_ref, far_out_ref, sems):
    tile, me = lax.axis_index("tile"), lax.axis_index("slide")
    owner = lax.rem(tile, 4) != 3
    unit = jnp.minimum((tile // 4) * 3 + lax.rem(tile, 4), UNITS - 1)

    @pl.loop(0, UNITS)
    def _(j):
        peer = owner_of(j)

        @pl.when(peer != tile)
        def _():
            pltpu.make_async_remote_copy(
                unit_at(flat_ref, j), near_ref.at[tile], sems.at[0], sems.at[1],
                device_id={"tile": peer}, device_id_type=MESH).start()

    def wait_units(ref, count, sem):
        some = pl.ds(0, count)
        pltpu.make_async_copy(ref.at[some], ref.at[some], sem).wait()

    @pl.when(owner)
    def _():
        near_ref[tile] = unit_at(flat_ref, unit)[...]
        wait_units(near_ref, PLANE - 1, sems.at[1])
        wait_units(near_ref, UNITS - 1, sems.at[0])
        near = jnp.sum(near_ref[...].astype(F32), axis=0).astype(BF)
        far_out_ref[0] = near
        far_ref[me] = near

        @pl.loop(1, SLIDES)
        def _(j):
            pltpu.make_async_remote_copy(
                far_out_ref.at[0], far_ref.at[me], sems.at[2], sems.at[3],
                device_id={"slide": shift(me, j, SLIDES)}, device_id_type=MESH).start()

        wait_units(far_ref, SLIDES - 1, sems.at[3])
        far_out_ref[1] = jnp.sum(far_ref[...].astype(F32), axis=0).astype(BF)
        pltpu.make_async_copy(far_out_ref.at[1], unit_at(res_ref, unit), sems.at[5]).start()

        @pl.loop(1, PLANE)
        def _(j):
            pltpu.make_async_remote_copy(
                far_out_ref.at[1], unit_at(res_ref, unit), sems.at[4], sems.at[5],
                device_id={"tile": shift(tile, j, PLANE)}, device_id_type=MESH).start()

        wait_units(far_ref, SLIDES - 1, sems.at[2])
        wait_units(near_ref, PLANE - 1, sems.at[4])

    @pl.when(jnp.logical_not(owner))
    def _():
        wait_units(near_ref, UNITS, sems.at[0])

    pltpu.make_async_copy(res_ref, res_ref, sems.at[5]).wait()


def sum_kernel(part_ref, kernel_ref, norm_ref, flat_ref, near_ref, far_ref, res_ref, far_out_ref, sems):
    greet(True)
    flat_ref[...] = part_ref[...].astype(BF)
    reduce_all(flat_ref, near_ref, far_ref, res_ref, far_out_ref, sems)
    result = res_ref[...].astype(F32)
    kernel_ref[...] = result[:49]
    norm_ref[...] = result[49:51]


VMEM_LIMIT = 60 * 1024 * 1024


def params(collective_id=None):
    if collective_id is None:
        return pltpu.CompilerParams(vmem_limit_bytes=VMEM_LIMIT)
    return pltpu.CompilerParams(
        vmem_limit_bytes=VMEM_LIMIT, collective_id=collective_id, has_side_effects=True)


def vmem(count):
    return [pl.BlockSpec(memory_space=pltpu.VMEM)] * count


def smem(count):
    return [pl.BlockSpec(memory_space=pltpu.SMEM)] * count


def shape(*dims, kind=BF):
    return jax.ShapeDtypeStruct(dims, kind)


def body(
    tile_maps, dw_kernel, conv_bias, norm_gain, w_in, w_qkv, seg_len, dilation,
    tile_slot, slide_lengths, cotangent,
):
    bias, gain = conv_bias.reshape(1, C), norm_gain.reshape(1, C)
    maps, normed, inverse, total, embed = pl.pallas_call(
        forward_kernel,
        out_shape=[
            shape(SIDE, SIDE, ROWS, C), shape(AREA, ROWS, C), shape(AREA, ROWS, LANE, kind=F32),
            shape(ROWS, C, kind=F32), shape(ROWS, C),
        ],
        in_specs=vmem(5),
        out_specs=vmem(5),
        scratch_shapes=[pltpu.VMEM((49, ROWS, C), BF), pltpu.VMEM((AREA, ROWS, C), F32)],
        compiler_params=params(),
    )(tile_maps, dw_kernel, bias, gain, w_in)
    dma = pltpu.SemaphoreType.DMA
    message = pltpu.VMEM((SLIDES, PACK, LANE), BF)
    attn_out, dpool = pl.pallas_call(
        owner_kernel,
        out_shape=[shape(ROWS, C), shape(ROWS, C, kind=F32)],
        in_specs=vmem(3) + smem(4) + vmem(1),
        out_specs=vmem(2),
        scratch_shapes=[
            pltpu.VMEM((3, HEADS, HEAD, C), BF), message, message, message, message,
            dma((9,)), dma((9,)), dma((9,)), dma((9,)), dma((2, 9)), dma((2, 9)), dma((4,)),
        ],
        compiler_params=params(1),
    )(embed, w_in, w_qkv.T, seg_len, dilation, tile_slot, slide_lengths, cotangent)
    part = pl.pallas_call(
        backward_kernel,
        out_shape=shape(SUM_ROWS, C, kind=F32),
        in_specs=vmem(6),
        out_specs=pl.BlockSpec(memory_space=pltpu.VMEM),
        scratch_shapes=[pltpu.VMEM((AREA, ROWS, C), BF)],
        compiler_params=params(),
    )(dpool, gain, maps, normed, inverse, total)
    grad_kernel, grad_norm = pl.pallas_call(
        sum_kernel,
        out_shape=[shape(49, C, kind=F32), shape(2, C, kind=F32)],
        in_specs=vmem(1),
        out_specs=vmem(2),
        scratch_shapes=[
            pltpu.VMEM((SUM_ROWS, C), BF), pltpu.VMEM((PLANE, 16, LANE), BF),
            pltpu.VMEM((SLIDES, 16, LANE), BF), pltpu.VMEM((SUM_ROWS, C), BF),
            pltpu.VMEM((2, 16, LANE), BF), dma((6,)),
        ],
        compiler_params=params(2),
    )(part)
    return attn_out, grad_kernel, grad_norm


def solution(mesh):
    both = ("tile", "slide")
    in_specs = (
        P(both, None, None, None), P(), P(), P(), P(), P(None, "slide"), P(), P(),
        P(both), P(both, None), P(both, None),
    )
    out_specs = (P(both, None), P(), P())
    return jax.shard_map(body, mesh=mesh, in_specs=in_specs, out_specs=out_specs, check_vma=False)
```

time: 616 us -> 142 us (0.23)
  waiting for transfers between devices: 381 us -> 0 us
  Pallas kernels: 0 us -> 135 us
  blocking collectives: 111 us -> 0 us
  other arithmetic: 38.4 us -> 0 us
  starting transfers between devices: 34.3 us -> 0 us
  matrix products: 20.9 us -> 0 us
  between operations: 14.8 us -> 0.66 us
  local copies, waits for them, and re-layouts: 14.6 us -> 6.05 us
    psum x1 -> x0, waiting for transfers between devices: 344 us -> none  [body(): lax.psum((kernel_part, norm_part), ('tile', 'slide'))]
    pallas_call x0 -> x4, Pallas kernels: none -> 135 us  [the longest x1 68.8 us: body(): pl.pallas_call(owner_kernel, out_shape=[shape(ROWS, C), shape(ROWS, C, ki...]
    psum x1 -> x0, blocking collectives: 111 us -> none  [body(): lax.psum((kernel_part, norm_part), ('tile', 'slide'))]
    all_to_all x3 -> x0, starting transfers between devices: 34 us -> none  [the longest x1 15.7 us: body(): lax.all_to_all(carried.reshape(devices, quota), 'slide', split_axis=0, co...]
    reduce_sum x11 -> x0, other arithmetic: 33 us -> none  [the longest x2 20.7 us: tile_grads(): jnp.sum(padded[:, row_off:row_off + side, col_off:col_off + side, :].asty...]
    all_to_all x3 -> x0, waiting for transfers between devices: 20.5 us -> none  [the longest x1 11.9 us: body(): lax.all_to_all(outgoing.reshape(devices, quota, width), 'slide', split_ax...]
    all_gather x1 -> x0, waiting for transfers between devices: 16.2 us -> none  [body(): full = lax.all_gather(w_qkv, 'slide', axis=1, tiled=True)]
    conv_general_dilated x1 -> x0, matrix products: 12.6 us -> none  [encode(): lax.conv_general_dilated(tile_maps, dw_kernel.reshape(7, 7, 1, channels),...]
  transfers between devices with their start and end apart: 5 -> 0, of which waited for: 4 -> 0; matrix products, arithmetic and copies ran while one was open for 4% -> 0% of each run, Pallas kernels for 0% -> 0%
where the time goes in v1:
time: 142 us; the launch traced here: 141 us
  Pallas kernels  135 us (95%)
  local copies, waits for them, and re-layouts  6.05 us (4%)
    pallas_call x1, Pallas kernels, body(): pl.pallas_call(owner_kernel, out_shape=[shape(ROWS, C), shape(ROWS, C, ki...  68.8 us
    pallas_call x1, Pallas kernels, body(): pl.pallas_call(sum_kernel, out_shape=[shape(49, C, kind=F32), shape(2, C,...  29.4 us
    pallas_call x1, Pallas kernels, body(): pl.pallas_call(forward_kernel, out_shape=[shape(SIDE, SIDE, ROWS, C), sha...  19.5 us
    pallas_call x1, Pallas kernels, body(): pl.pallas_call(backward_kernel, out_shape=shape(SUM_ROWS, C, kind=F32), i...  16.8 us
    unnamed x5, local copies, waits for them, and re-layouts  3.5 us

profile of v1, /device:TPU:1, one launch (start us, length us, event | category | flops | bytes accessed | tf_op | source)
XLA Modules:
  0.0 141.2 jit_solution(2188251272945597203)
XLA Ops:
  0.6 1.3 reshape.12.bias_ref
  1.9 1.3 reshape.13.gain_ref
  3.2 19.5 %shard_map.130 = (bf16[8,8,16,768]{3,2,1,0:T(8,128)(2,1)}, bf16[64,16,768]{2,1,0:T(8,128)(2,1)}, f32[64,16,128]{2,1,0:T(8,128)}, f32[16,768]{1,0:T(8,128)}, bf16[16,768]{1,0:T(8,128)(2,1)}) custom-call(bf16[16,8,8,768]{3,2,1,0:T(8,128)(2,1)} %maps_ref.1, bf16[49,768]{1,0:T(8,128)(2,1)} %dw_ref.1, f32[1,768]{1,0:T(1,128)} %reshape.12.bias_ref, ...), custom_call_target="tpu_custom_call" | custom-call | tf_op jit(solution)/shard_map/pallas_call | solution.py:512
  22.7 68.8 %shard_map.131 = (bf16[16,768]{1,0:T(8,128)(2,1)}, f32[16,768]{1,0:T(8,128)}) custom-call(bf16[16,768]{1,0:T(8,128)(2,1)} %get-tuple-element.12.embed_ref, bf16[768,768]{1,0:T(8,128)(2,1)} %win_ref.3, bf16[144,768]{1,0:T(8,128)(2,1)} %bitcast.1, s32[16]{0:T(128)} %seg_ref.1, s32[16]{0:T(128)} %dil_ref.1, s32[16]{0:T(128)} %slot_ref.1, s32[1,2]{1,0:T(1,128)} %len_ref.1, ...), custom_call_target="tpu_custom_call" | custom-call | tf_op jit(solution)/shard_map/pallas_call | solution.py:525
  91.5 0.0 copy-start
  91.5 16.8 %shard_map.132.part_ref = f32[64,768]{1,0:T(8,128)} custom-call(f32[16,768]{1,0:T(8,128)} %get-tuple-element.14.dpool_ref, f32[1,768]{1,0:T(1,128)} %reshape.13.gain_ref, bf16[8,8,16,768]{3,2,1,0:T(8,128)(2,1)} %get-tuple-element.15.xt_ref, bf16[64,16,768]{2,1,0:T(8,128)(2,1)} %get-tuple-element.16.nrm_ref, f32[64,16,128]{2,1,0:T(8,128)} %get-tuple-element.17.inv_ref, ...), custom_call_target="tpu_custom_call" | custom-call | tf_op jit(solution)/shard_map/pallas_call | solution.py:536
  108.3 29.4 %shard_map.133 = (f32[49,768]{1,0:T(8,128)}, f32[2,768]{1,0:T(2,128)}) custom-call(f32[64,768]{1,0:T(8,128)} %shard_map.132.part_ref), custom_call_target="tpu_custom_call" | custom-call | tf_op jit(solution)/shard_map/pallas_call | solution.py:544
  137.7 0.0 copy-done
  137.7 0.6 copy.17
  138.3 1.6 %copy.18 = f32[49,768]{1,0:T(8,128)} copy(f32[49,768]{1,0:T(8,128)} %get-tuple-element.25) | data formatting | bytes 301056
  139.9 1.3 copy.19
Async XLA Ops:
  91.5 46.2 %copy-start = (bf16[16,768]{1,0:T(8,128)(2,1)S(1)}, bf16[16,768]{1,0:T(8,128)(2,1)}, u32[]{:S(2)}) copy-start(bf16[16,768]{1,0:T(8,128)(2,1)} %get-tuple-element.24) | copy-start | bytes 73732

commit v2 on v1

v2 whole, which is shorter than its diff:
```python
import jax
import jax.numpy as jnp
from jax import lax
from jax.experimental import pallas as pl
from jax.experimental.pallas import tpu as pltpu
from jax.sharding import PartitionSpec as P

NORM_EPS = 1e-06
MESH = pl.DeviceIdType.MESH
BF = jnp.bfloat16
F32 = jnp.float32

SIDE = 8
AREA = SIDE * SIDE
REACH = 3
TAPS = 7
ROWS = 16
C = 768
LANE = 128
CHUNKS = C // LANE
HEADS = 16
HEAD = 48
SLIDES = 16
PLANE = 32
QUOTA = 3
PACK = 32
HALF = C // 2
UNITS = 24
SUM_ROWS = 64


def iota(shape, dim):
    return lax.broadcasted_iota(jnp.int32, shape, dim)


def dot(left, right):
    return jnp.dot(left, right, preferred_element_type=F32)


def dot_last(left, right):
    return lax.dot_general(left, right, (((1,), (1,)), ((), ())), preferred_element_type=F32)


def dot_first(left, right):
    return lax.dot_general(left, right, (((0,), (0,)), ((), ())), preferred_element_type=F32)


def spread(block):
    return jnp.concatenate([block[:, k * LANE : (k + 1) * LANE] for k in range(CHUNKS)], axis=0)


def gather_chunks(stack):
    return jnp.concatenate([stack[k * ROWS : (k + 1) * ROWS] for k in range(CHUNKS)], axis=1)


def row_span(offset):
    return max(0, -offset), min(SIDE, SIDE - offset)


def map_copy(maps_ref, rows_ref, sems, r):
    return pltpu.make_async_copy(maps_ref.at[:, r], rows_ref.at[r], sems.at[r])


def transpose_maps(maps_ref, rows_ref, sems, xt_ref):
    row, col = iota((128, 128), 0), iota((128, 128), 1)
    perm = ((row >> 4) == (col & 7)) & ((row & 15) == (col >> 3))
    perm = perm.astype(F32).astype(BF)
    for r in range(SIDE):
        map_copy(maps_ref, rows_ref, sems, r).wait()
        part = rows_ref[r].astype(F32).reshape(128, C).astype(BF)
        xt_ref[r] = dot(perm, part).reshape(SIDE, ROWS, C)


def spread_taps(dw_ref, wb_ref):
    taps = dw_ref[...].astype(F32)
    for tap in range(TAPS * TAPS):
        wb_ref[tap] = jnp.broadcast_to(taps[tap : tap + 1], (8, C))


def conv_chunk(chunk, xt_ref, wb_ref, bias_ref, cv_ref):
    lanes = pl.ds(pl.multiple_of(chunk * LANE, LANE), LANE)
    bias = jnp.broadcast_to(bias_ref[lanes].reshape(1, LANE), (2, 8, LANE))
    for i in range(SIDE):
        total = [bias] * SIDE
        for r in range(TAPS):
            src = i + r - REACH
            if not 0 <= src < SIDE:
                continue
            cells = [xt_ref[src, j, :, lanes].reshape(2, 8, LANE) for j in range(SIDE)]
            taps = [wb_ref[r * TAPS + s, :, lanes] for s in range(TAPS)]
            for j in range(SIDE):
                for s in range(TAPS):
                    at = j + s - REACH
                    if 0 <= at < SIDE:
                        total[j] = total[j] + cells[at] * taps[s]
        for j in range(SIDE):
            cv_ref[i * SIDE + j, :, lanes] = total[j].reshape(ROWS, LANE)


def normalise(cv_ref, inv_ref, rows, total):
    def step(b, total):
        some = pl.ds(b * SIDE, SIDE)
        mean = jnp.mean(cv_ref[some], axis=2, keepdims=True)
        centered = cv_ref[some] - mean
        inv = lax.rsqrt(jnp.mean(centered * centered, axis=2, keepdims=True) + NORM_EPS)
        normed = (cv_ref[some] - mean) * inv
        cv_ref[some] = normed
        inv_ref[some] = jnp.broadcast_to(inv, (SIDE, ROWS, LANE))
        return total + jnp.sum(normed, axis=0)

    return lax.fori_loop(rows[0], rows[1], step, total)


def send_rows(slot_ref):
    lane = iota((1, 112), 1)
    tile, chunk = lane & 15, lane >> 4
    owner = jnp.zeros((1, 112), jnp.int32)
    for t in range(ROWS):
        owner = jnp.where(tile == t, slot_ref[t] >> 4, owner)
    rank = jnp.zeros((1, 112), jnp.int32)
    for t in range(ROWS):
        rank = rank + jnp.where((owner == (slot_ref[t] >> 4)) & (tile > t), 1, 0)
    want = owner * PACK + chunk * QUOTA + rank
    select = (iota((SLIDES * PACK, 112), 0) == want).astype(F32).astype(BF)
    sub = iota((ROWS, LANE), 0)
    slots = jnp.zeros((ROWS, LANE), jnp.int32)
    for t in range(ROWS):
        slots = jnp.where(sub == t, (slot_ref[t] & 15) + 1, slots)
    return select, slots.astype(F32).astype(BF)


def slot_spread():
    size = SLIDES * PACK
    row, col = iota((size, size), 0), iota((size, size), 1)
    inside = row & (PACK - 1)
    quota = inside
    for k in range(1, PACK // QUOTA + 1):
        quota = jnp.where(inside >= k * QUOTA, inside - k * QUOTA, quota)
    return (col == (row - inside + CHUNKS * QUOTA + quota)).astype(F32).astype(BF)


def place_rows(spread_slots, arrived):
    size = SLIDES * PACK
    slot = dot(spread_slots, arrived)[:, : CHUNKS * ROWS]
    inside = iota((size, CHUNKS * ROWS), 0) & (PACK - 1)
    lane = iota((size, CHUNKS * ROWS), 1)
    first = (lane >> 4) * QUOTA
    want = ((lane & 15) + 1).astype(F32)
    hit = (inside >= first) & (inside < first + QUOTA) & (slot == want)
    return hit.astype(F32).astype(BF)


def head_mask():
    row, lane = iota((HEADS * ROWS, C), 0), iota((HEADS * ROWS, C), 1)
    low = (row >> 4) * HEAD
    return ((lane >= low) & (lane < low + HEAD)).astype(F32).astype(BF)


def allowed_pairs(seg_ref, dil_ref, len_ref):
    left, right = iota((ROWS, ROWS), 0), iota((ROWS, ROWS), 1)
    cut = len_ref[0, 0]
    run_left, run_right = left >= cut, right >= cut
    pos_left = jnp.where(run_left, left - cut, left)
    pos_right = jnp.where(run_right, right - cut, right)
    apart = pos_left ^ pos_right
    apart = jnp.where(run_left != run_right, apart | 256, apart)
    parts = []
    for h in range(HEADS):
        parts.append(apart & (~(seg_ref[h] - 1) | (dil_ref[h] - 1)))
    return jnp.concatenate(parts, axis=0) == 0


def attention(block, w3_ref, cot_ref, attn_ref, mask, allowed):
    scale = HEAD ** (-0.5)
    weights = [w3_ref[part].reshape(C, C) for part in range(3)]
    query, key, value = [dot_last(block, each).astype(BF) for each in weights]
    many_query = jnp.concatenate([query] * HEADS, axis=0) * mask
    many_grad = jnp.concatenate([cot_ref[...]] * HEADS, axis=0) * mask
    scores = dot_last(many_query, key) * scale
    masked = jnp.where(allowed, scores, -1e30)
    top = jnp.max(masked, axis=1, keepdims=True)
    expo = jnp.where(allowed, jnp.exp(masked - top), 0.0)
    prob = expo / jnp.sum(expo, axis=1, keepdims=True)
    prob_bf = prob.astype(BF)
    mask_f = mask.astype(F32)

    def own_head(full):
        return jnp.sum((full * mask_f).reshape(HEADS, ROWS, C), axis=0)

    attn_ref[...] = own_head(dot(prob_bf, value)).astype(BF)
    dprob = dot_last(many_grad, value)
    dscore = (prob * (dprob - jnp.sum(prob * dprob, axis=1, keepdims=True)) * scale).astype(BF)
    dquery = own_head(dot(dscore, key)).astype(BF)
    dkey = dot_first(dscore, many_query).astype(BF)
    dvalue = dot_first(prob_bf, many_grad).astype(BF)
    total = dot(dquery, weights[0]) + dot(dkey, weights[1]) + dot(dvalue, weights[2])
    return total.astype(BF)


def shift(index, by, size):
    return (index + by + size) & (size - 1)


def core_of(tile):
    return tile & 1


class Ring:
    def __init__(self, w3_ref, sems):
        self.w3_ref = w3_ref
        self.right, self.left, self.core = sems[0:2], sems[2:4], sems[4:6]
        tile = lax.axis_index("tile")
        self.me = lax.axis_index("slide")
        self.lanes = pl.ds(pl.multiple_of(core_of(tile) * HALF, HALF), HALF)
        self.other = tile + 1 - 2 * core_of(tile)

    def copy(self, head, send_sem, recv_sem, device):
        block = self.w3_ref.at[:, head, :, self.lanes]
        return pltpu.make_async_remote_copy(
            block, block, send_sem, recv_sem, device_id=device, device_id_type=MESH)

    def to_right(self, s):
        return self.copy(
            shift(self.me, -s, SLIDES), self.right[0].at[s], self.right[1].at[s],
            {"slide": shift(self.me, 1, SLIDES)})

    def to_left(self, s):
        return self.copy(
            shift(self.me, s, SLIDES), self.left[0].at[s], self.left[1].at[s],
            {"slide": shift(self.me, -1, SLIDES)})

    def left_to_core(self, s):
        return self.copy(
            shift(self.me, -s, SLIDES), self.core[0].at[0, s], self.core[1].at[0, s],
            {"tile": self.other})

    def right_to_core(self, s):
        return self.copy(
            shift(self.me, s, SLIDES), self.core[0].at[1, s], self.core[1].at[1, s],
            {"tile": self.other})


RIGHT_STEPS = SLIDES // 2
LEFT_STEPS = SLIDES // 2 - 1


def ring_start(wq_ref, w3_ref, ring):
    w3_ref[:, ring.me] = wq_ref[...].reshape(3, HEAD, C)
    ring.to_right(0).start()
    ring.to_left(0).start()


def ring_step(ring, s, inner=False):
    ring.to_right(s - 1).wait_recv()
    if inner or s < RIGHT_STEPS:
        ring.to_right(s).start()
    ring.left_to_core(s).start()
    if inner or s <= LEFT_STEPS:
        ring.to_left(s - 1).wait_recv()
        if inner or s < LEFT_STEPS:
            ring.to_left(s).start()
        ring.right_to_core(s).start()


def ring_end(ring):
    for s in range(RIGHT_STEPS + 1):
        if s >= 1:
            ring.left_to_core(s).wait()
        if 1 <= s <= LEFT_STEPS:
            ring.right_to_core(s).wait()
        if s < RIGHT_STEPS:
            ring.to_right(s).wait_send()
        if s < LEFT_STEPS:
            ring.to_left(s).wait_send()


def exchange_start(out_ref, in_ref, send_sem, recv_sem):
    me = lax.axis_index("slide")
    in_ref[me] = out_ref[me]

    @pl.loop(1, SLIDES)
    def _(j):
        peer = shift(me, j, SLIDES)
        pltpu.make_async_remote_copy(
            out_ref.at[peer], in_ref.at[me], send_sem, recv_sem,
            device_id={"slide": peer}, device_id_type=MESH).start()


def exchange_wait(out_ref, in_ref, send_sem, recv_sem):
    some = pl.ds(0, SLIDES - 1)
    pltpu.make_async_copy(in_ref.at[some], in_ref.at[some], recv_sem).wait()
    pltpu.make_async_copy(out_ref.at[some], out_ref.at[some], send_sem).wait()


def greet():
    tile, me = lax.axis_index("tile"), lax.axis_index("slide")
    barrier = pltpu.get_barrier_semaphore()

    @pl.loop(1, SLIDES)
    def _(j):
        pl.semaphore_signal(
            barrier, inc=1, device_id={"slide": shift(me, j, SLIDES)}, device_id_type=MESH)

    @pl.loop(1, PLANE)
    def _(j):
        pl.semaphore_signal(
            barrier, inc=1, device_id={"tile": shift(tile, j, PLANE)}, device_id_type=MESH)


def greeted():
    pl.semaphore_wait(pltpu.get_barrier_semaphore(), SLIDES + PLANE - 2)


def conv_grads(dpool, gain, cv_ref, inv_ref):
    grad = dpool * (gain * (1.0 / AREA))
    level = grad - jnp.mean(grad, axis=1, keepdims=True)

    def step(b, total):
        some = pl.ds(b * SIDE, SIDE)
        along = jnp.mean(cv_ref[some] * grad, axis=2, keepdims=True)
        dconv = inv_ref[some][:, :, :1] * (level - cv_ref[some] * along)
        cv_ref[some] = dconv
        return total + jnp.sum(dconv, axis=0)

    return lax.fori_loop(0, SIDE, step, jnp.zeros((ROWS, C), F32))


def tap_grads(chunk, xt_ref, cv_ref, part_ref):
    lanes = pl.ds(pl.multiple_of(chunk * LANE, LANE), LANE)
    for r in range(TAPS):
        total = [jnp.zeros((ROWS, LANE), F32)] * TAPS
        for i in range(*row_span(r - REACH)):
            cells = [xt_ref[i + r - REACH, j, :, lanes] for j in range(SIDE)]
            grads = [cv_ref[i * SIDE + j, :, lanes] for j in range(SIDE)]
            for s in range(TAPS):
                for j in range(*row_span(s - REACH)):
                    total[s] = total[s] + cells[j + s - REACH] * grads[j]
        for s in range(TAPS):
            tap = r * TAPS + s
            part_ref[tap : tap + 1, lanes] = jnp.sum(total[s], axis=0, keepdims=True)


def unit_at(ref, unit):
    rows = pl.ds(pl.multiple_of((unit & 3) * 16, 16), 16)
    lanes = pl.ds(pl.multiple_of((unit >> 2) * LANE, LANE), LANE)
    return ref.at[rows, lanes]


def owner_of(unit):
    return unit + ((unit * 11) >> 5)


def reduce_all(flat_ref, near_ref, far_ref, res_ref, far_out_ref, sems):
    tile, me = lax.axis_index("tile"), lax.axis_index("slide")
    owner = (tile & 3) != 3
    unit = jnp.minimum((tile >> 2) * 3 + (tile & 3), UNITS - 1)

    @pl.loop(0, UNITS)
    def _(j):
        peer = owner_of(j)

        @pl.when(peer != tile)
        def _():
            pltpu.make_async_remote_copy(
                unit_at(flat_ref, j), near_ref.at[tile], sems.at[0], sems.at[1],
                device_id={"tile": peer}, device_id_type=MESH).start()

    def wait_units(ref, count, sem):
        some = pl.ds(0, count)
        pltpu.make_async_copy(ref.at[some], ref.at[some], sem).wait()

    @pl.when(owner)
    def _():
        near_ref[tile] = unit_at(flat_ref, unit)[...]
        wait_units(near_ref, PLANE - 1, sems.at[1])
        wait_units(near_ref, UNITS - 1, sems.at[0])
        near = jnp.sum(near_ref[...].astype(F32), axis=0).astype(BF)
        far_out_ref[0] = near
        far_ref[me] = near

        @pl.loop(1, SLIDES)
        def _(j):
            pltpu.make_async_remote_copy(
                far_out_ref.at[0], far_ref.at[me], sems.at[2], sems.at[3],
                device_id={"slide": shift(me, j, SLIDES)}, device_id_type=MESH).start()

        wait_units(far_ref, SLIDES - 1, sems.at[3])
        far_out_ref[1] = jnp.sum(far_ref[...].astype(F32), axis=0).astype(BF)
        pltpu.make_async_copy(far_out_ref.at[1], unit_at(res_ref, unit), sems.at[5]).start()

        @pl.loop(1, PLANE)
        def _(j):
            pltpu.make_async_remote_copy(
                far_out_ref.at[1], unit_at(res_ref, unit), sems.at[4], sems.at[5],
                device_id={"tile": shift(tile, j, PLANE)}, device_id_type=MESH).start()

        wait_units(far_ref, SLIDES - 1, sems.at[2])
        wait_units(near_ref, PLANE - 1, sems.at[4])

    @pl.when(jnp.logical_not(owner))
    def _():
        wait_units(near_ref, UNITS, sems.at[0])

    pltpu.make_async_copy(res_ref, res_ref, sems.at[5]).wait()


def step_kernel(
    maps_ref, dw_ref, bias_ref, gain_ref, win_hbm, wq_ref, seg_ref, dil_ref, slot_ref, len_ref, cot_ref,
    attn_ref, sums_ref,
    rows_ref, xt_ref, cv_ref, inv_ref, wb_ref, win_ref, w3_ref,
    out_ref, in_ref, back_out_ref, back_in_ref,
    part_ref, flat_ref, near_ref, far_ref, far_out_ref, res_ref,
    local_sems, right_send, right_recv, left_send, left_recv, core_send, core_recv, route_sems, sum_sems,
):
    greet()
    for r in range(SIDE):
        map_copy(maps_ref, rows_ref, local_sems, r).start()
    win_copy = pltpu.make_async_copy(win_hbm, win_ref, local_sems.at[SIDE])
    win_copy.start()
    ring = Ring(w3_ref, (right_send, right_recv, left_send, left_recv, core_send, core_recv))
    w3_ref[:, ring.me] = wq_ref[...].reshape(3, HEAD, C)
    spread_taps(dw_ref, wb_ref)
    greeted()
    ring.to_right(0).start()
    ring.to_left(0).start()
    transpose_maps(maps_ref, rows_ref, local_sems, xt_ref)

    @pl.loop(0, 2)
    def _(half):
        @pl.loop(0, CHUNKS // 2)
        def _(chunk):
            conv_chunk(half * (CHUNKS // 2) + chunk, xt_ref, wb_ref, bias_ref, cv_ref)

        ring_step(ring, half + 1, True)

    total = normalise(cv_ref, inv_ref, (0, SIDE), jnp.zeros((ROWS, C), F32))
    ring_step(ring, 3)
    gain = gain_ref[...].reshape(1, C)
    pooled = (total * gain * (1.0 / AREA)).astype(BF)
    win_copy.wait()
    embed = dot(pooled, win_ref[...]).astype(BF)

    select, slots = send_rows(slot_ref)
    packed = jnp.concatenate([spread(embed), slots], axis=0)
    out_ref[...] = dot(select, packed).astype(BF).reshape(SLIDES, PACK, LANE)
    exchange_start(out_ref, in_ref, route_sems.at[0], route_sems.at[1])
    spread_slots, mask = slot_spread(), head_mask()
    allowed = allowed_pairs(seg_ref, dil_ref, len_ref)
    for s in range(4, RIGHT_STEPS + 1):
        ring_step(ring, s)
    exchange_wait(out_ref, in_ref, route_sems.at[0], route_sems.at[1])
    arrived = in_ref[...].reshape(SLIDES * PACK, LANE)
    place = place_rows(spread_slots, arrived)
    block = gather_chunks(dot_first(place, arrived).astype(BF))
    ring_end(ring)
    dblock = attention(block, w3_ref, cot_ref, attn_ref, mask, allowed)
    back_out_ref[...] = dot(place, spread(dblock)).astype(BF).reshape(SLIDES, PACK, LANE)
    exchange_start(back_out_ref, back_in_ref, route_sems.at[2], route_sems.at[3])
    exchange_wait(back_out_ref, back_in_ref, route_sems.at[2], route_sems.at[3])
    returned = back_in_ref[...].reshape(SLIDES * PACK, LANE)
    dembed = gather_chunks(dot_first(select[:, : CHUNKS * ROWS], returned).astype(BF))
    dpool = dot_last(dembed, win_ref[...])

    bias_grad = conv_grads(dpool, gain, cv_ref, inv_ref)
    part_ref[...] = jnp.zeros(part_ref.shape, F32)
    part_ref[49:50] = jnp.sum(bias_grad, axis=0, keepdims=True)
    part_ref[50:51] = jnp.sum(dpool * total, axis=0, keepdims=True) * (1.0 / AREA)

    @pl.loop(0, CHUNKS)
    def _(chunk):
        tap_grads(chunk, xt_ref, cv_ref, part_ref)

    flat_ref[...] = part_ref[...].astype(BF)
    reduce_all(flat_ref, near_ref, far_ref, res_ref, far_out_ref, sum_sems)
    sums_ref[...] = res_ref[...]


def finish_kernel(attn_ref, res_ref, out_ref, kernel_ref, norm_ref):
    out_ref[...] = attn_ref[...]
    result = res_ref[...].astype(F32)
    kernel_ref[...] = result[:49]
    norm_ref[...] = result[49:51]


VMEM_LIMIT = 60 * 1024 * 1024


def params(**extra):
    return pltpu.CompilerParams(vmem_limit_bytes=VMEM_LIMIT, **extra)


def vmem(count):
    return [pl.BlockSpec(memory_space=pltpu.VMEM)] * count


def smem(count):
    return [pl.BlockSpec(memory_space=pltpu.SMEM)] * count


def shape(*dims, kind=BF):
    return jax.ShapeDtypeStruct(dims, kind)


def body(
    tile_maps, dw_kernel, conv_bias, norm_gain, w_in, w_qkv, seg_len, dilation,
    tile_slot, slide_lengths, cotangent,
):
    dma = pltpu.SemaphoreType.DMA
    hbm = [pl.BlockSpec(memory_space=pl.ANY)]
    message = pltpu.VMEM((SLIDES, PACK, LANE), BF)
    attn, sums = pl.pallas_call(
        step_kernel,
        out_shape=[shape(ROWS, C), shape(SUM_ROWS, C)],
        in_specs=hbm + vmem(3) + hbm + vmem(1) + smem(4) + vmem(1),
        out_specs=vmem(2),
        scratch_shapes=[
            pltpu.VMEM((SIDE, ROWS, SIDE, C), BF), pltpu.VMEM((SIDE, SIDE, ROWS, C), F32),
            pltpu.VMEM((AREA, ROWS, C), F32), pltpu.VMEM((AREA, ROWS, LANE), F32),
            pltpu.VMEM((49, 8, C), F32), pltpu.VMEM((C, C), BF),
            pltpu.VMEM((3, HEADS, HEAD, C), BF), message, message, message, message,
            pltpu.VMEM((SUM_ROWS, C), F32), pltpu.VMEM((SUM_ROWS, C), BF),
            pltpu.VMEM((PLANE, 16, LANE), BF), pltpu.VMEM((SLIDES, 16, LANE), BF),
            pltpu.VMEM((2, 16, LANE), BF), pltpu.VMEM((SUM_ROWS, C), BF),
            dma((9,)), dma((9,)), dma((9,)), dma((9,)), dma((9,)), dma((2, 9)), dma((2, 9)), dma((4,)),
            dma((6,)),
        ],
        compiler_params=params(collective_id=1, has_side_effects=True),
    )(
        tile_maps, dw_kernel, conv_bias, norm_gain, w_in, w_qkv.T,
        seg_len, dilation, tile_slot, slide_lengths, cotangent,
    )
    return pl.pallas_call(
        finish_kernel,
        out_shape=[shape(ROWS, C), shape(49, C, kind=F32), shape(2, C, kind=F32)],
        in_specs=vmem(2),
        out_specs=vmem(3),
    )(attn, sums)


def solution(mesh):
    both = ("tile", "slide")
    in_specs = (
        P(both, None, None, None), P(), P(), P(), P(), P(None, "slide"), P(), P(),
        P(both), P(both, None), P(both, None),
    )
    out_specs = (P(both, None), P(), P())
    return jax.shard_map(body, mesh=mesh, in_specs=in_specs, out_specs=out_specs, check_vma=False)
```

time: 142 us -> 106 us (0.75)
  Pallas kernels: 135 us -> 106 us
  local copies, waits for them, and re-layouts: 6.05 us -> 0 us
    pallas_call x4 -> x2, Pallas kernels: 135 us -> 106 us  [the longest x1 104 us: body(): pl.pallas_call(step_kernel, out_shape=[shape(ROWS, C), shape(SUM_ROWS, C)...]
    unnamed x5 -> x0, local copies, waits for them, and re-layouts: 3.5 us -> none
    reshape x2 -> x0, local copies, waits for them, and re-layouts: 2.55 us -> none  [body(): bias, gain = (conv_bias.reshape(1, C), norm_gain.reshape(1, C))]
where the time goes in v2:
time: 106 us
  Pallas kernels  106 us (100%)
    pallas_call x1, Pallas kernels, body(): pl.pallas_call(step_kernel, out_shape=[shape(ROWS, C), shape(SUM_ROWS, C)...  104 us

profile of v2, /device:TPU:1, one launch (start us, length us, event | category | flops | bytes accessed | tf_op | source)
XLA Modules:
  0.0 106.3 jit_solution(11826575495472281640)
XLA Ops:
  0.6 104.1 %shard_map.130 = (bf16[16,768]{1,0:T(8,128)(2,1)}, bf16[64,768]{1,0:T(8,128)(2,1)}) custom-call(bf16[16,8,8,768]{3,2,1,0:T(8,128)(2,1)} %maps_ref.1, bf16[49,768]{1,0:T(8,128)(2,1)} %dw_ref.1, f32[768]{0:T(1024)} %bias_ref.1, f32[768]{0:T(1024)} %gain_ref.1, bf16[768,768]{1,0:T(8,128)(2,1)} %win_hbm.1, bf16[144,768]{1,0:T(8,128)(2,1)} %bitcast.1, ...), custom_call_target="tpu_custom_call" | custom-call | tf_op jit(solution)/shard_map/pallas_call | solution.py:511
  104.7 1.6 %shard_map.131 = (bf16[16,768]{1,0:T(8,128)(2,1)}, f32[49,768]{1,0:T(8,128)}, f32[2,768]{1,0:T(2,128)}) custom-call(bf16[16,768]{1,0:T(8,128)(2,1)} %get-tuple-element.5.attn_ref, bf16[64,768]{1,0:T(8,128)(2,1)} %get-tuple-element.6.res_ref), custom_call_target="tpu_custom_call" | custom-call | tf_op jit(solution)/shard_map/pallas_call | solution.py:532

commit v3 on v2

--- a/solution.py
+++ b/solution.py
@@ -24,7 +24,10 @@
 PLANE = 32
 QUOTA = 3
 PACK = 32
-HALF = C // 2
+MEMBERS = 8
+SHARE = HEADS // MEMBERS
+WIDE = MEMBERS * ROWS
+COLS = SHARE * HEAD
 UNITS = 24
 SUM_ROWS = 64
 
@@ -151,31 +154,42 @@
 
 
 def head_mask():
-    row, lane = iota((HEADS * ROWS, C), 0), iota((HEADS * ROWS, C), 1)
-    low = (row >> 4) * HEAD
+    row, lane = iota((SHARE * WIDE, COLS), 0), iota((SHARE * WIDE, COLS), 1)
+    low = jnp.where(row >= WIDE, HEAD, 0)
     return ((lane >= low) & (lane < low + HEAD)).astype(F32).astype(BF)
 
 
-def allowed_pairs(seg_ref, dil_ref, len_ref):
-    left, right = iota((ROWS, ROWS), 0), iota((ROWS, ROWS), 1)
-    cut = len_ref[0, 0]
-    run_left, run_right = left >= cut, right >= cut
-    pos_left = jnp.where(run_left, left - cut, left)
-    pos_right = jnp.where(run_right, right - cut, right)
+def member_columns():
+    row, col = iota((C, MEMBERS * LANE), 0), iota((C, MEMBERS * LANE), 1)
+    lane = col & (LANE - 1)
+    first = (col >> 7) * HEAD + lane
+    want = jnp.where(lane < HEAD, first, first + (MEMBERS - 1) * HEAD)
+    want = jnp.where(lane < COLS, want, -1)
+    return (row == want).astype(F32).astype(BF)
+
+
+def allowed_pairs(member, seg_ref, dil_ref, cut):
+    left, right = iota((WIDE, WIDE), 0), iota((WIDE, WIDE), 1)
+    slot_left, slot_right = left & 15, right & 15
+    run_left, run_right = slot_left >= cut, slot_right >= cut
+    pos_left = jnp.where(run_left, slot_left - cut, slot_left)
+    pos_right = jnp.where(run_right, slot_right - cut, slot_right)
     apart = pos_left ^ pos_right
     apart = jnp.where(run_left != run_right, apart | 256, apart)
+    apart = jnp.where((left >> 4) != (right >> 4), apart | 256, apart)
     parts = []
-    for h in range(HEADS):
-        parts.append(apart & (~(seg_ref[h] - 1) | (dil_ref[h] - 1)))
+    for h in range(SHARE):
+        seg, dil = seg_ref[member + MEMBERS * h], dil_ref[member + MEMBERS * h]
+        parts.append(apart & (~(seg - 1) | (dil - 1)))
     return jnp.concatenate(parts, axis=0) == 0
 
 
-def attention(block, w3_ref, cot_ref, attn_ref, mask, allowed):
+def attention(block, upstream, w3_ref, mask, allowed):
     scale = HEAD ** (-0.5)
-    weights = [w3_ref[part].reshape(C, C) for part in range(3)]
+    weights = [w3_ref[part].reshape(COLS, C) for part in range(3)]
     query, key, value = [dot_last(block, each).astype(BF) for each in weights]
-    many_query = jnp.concatenate([query] * HEADS, axis=0) * mask
-    many_grad = jnp.concatenate([cot_ref[...]] * HEADS, axis=0) * mask
+    many_query = jnp.concatenate([query] * SHARE, axis=0) * mask
+    many_grad = jnp.concatenate([upstream] * SHARE, axis=0) * mask
     scores = dot_last(many_query, key) * scale
     masked = jnp.where(allowed, scores, -1e30)
     top = jnp.max(masked, axis=1, keepdims=True)
@@ -185,93 +199,110 @@
     mask_f = mask.astype(F32)
 
     def own_head(full):
-        return jnp.sum((full * mask_f).reshape(HEADS, ROWS, C), axis=0)
-
-    attn_ref[...] = own_head(dot(prob_bf, value)).astype(BF)
+        return jnp.sum((full * mask_f).reshape(SHARE, WIDE, COLS), axis=0)
+
+    mixed = own_head(dot(prob_bf, value))
     dprob = dot_last(many_grad, value)
     dscore = (prob * (dprob - jnp.sum(prob * dprob, axis=1, keepdims=True)) * scale).astype(BF)
     dquery = own_head(dot(dscore, key)).astype(BF)
     dkey = dot_first(dscore, many_query).astype(BF)
     dvalue = dot_first(prob_bf, many_grad).astype(BF)
     total = dot(dquery, weights[0]) + dot(dkey, weights[1]) + dot(dvalue, weights[2])
-    return total.astype(BF)
+    return mixed, total
 
 
 def shift(index, by, size):
     return (index + by + size) & (size - 1)
 
 
-def core_of(tile):
-    return tile & 1
-
-
-class Ring:
-    def __init__(self, w3_ref, sems):
-        self.w3_ref = w3_ref
-        self.right, self.left, self.core = sems[0:2], sems[2:4], sems[4:6]
-        tile = lax.axis_index("tile")
-        self.me = lax.axis_index("slide")
-        self.lanes = pl.ds(pl.multiple_of(core_of(tile) * HALF, HALF), HALF)
-        self.other = tile + 1 - 2 * core_of(tile)
-
-    def copy(self, head, send_sem, recv_sem, device):
-        block = self.w3_ref.at[:, head, :, self.lanes]
+class Weights:
+    def __init__(self, w3_ref, send_sems, recv_sems, share_sems):
+        self.w3_ref, self.send, self.recv, self.share = w3_ref, send_sems, recv_sems, share_sems
+        self.tile, self.me = lax.axis_index("tile"), lax.axis_index("slide")
+        self.y = (self.tile >> 1) & 3
+        self.member = (self.tile >> 3) * 2 + (self.tile & 1)
+        self.carrier = self.y < 3
+        self.row = pl.multiple_of(jnp.minimum(self.y, 2) * 16, 16)
+        self.source = self.carrier & ((self.me & 7) == self.member)
+
+    def along_z(self, j):
+        head = self.me >> 3
+        rows = self.w3_ref.at[:, head, pl.ds(self.row, 16)]
         return pltpu.make_async_remote_copy(
-            block, block, send_sem, recv_sem, device_id=device, device_id_type=MESH)
-
-    def to_right(self, s):
-        return self.copy(
-            shift(self.me, -s, SLIDES), self.right[0].at[s], self.right[1].at[s],
-            {"slide": shift(self.me, 1, SLIDES)})
-
-    def to_left(self, s):
-        return self.copy(
-            shift(self.me, s, SLIDES), self.left[0].at[s], self.left[1].at[s],
-            {"slide": shift(self.me, -1, SLIDES)})
-
-    def left_to_core(self, s):
-        return self.copy(
-            shift(self.me, -s, SLIDES), self.core[0].at[0, s], self.core[1].at[0, s],
-            {"tile": self.other})
-
-    def right_to_core(self, s):
-        return self.copy(
-            shift(self.me, s, SLIDES), self.core[0].at[1, s], self.core[1].at[1, s],
-            {"tile": self.other})
-
-
-RIGHT_STEPS = SLIDES // 2
-LEFT_STEPS = SLIDES // 2 - 1
-
-
-def ring_start(wq_ref, w3_ref, ring):
-    w3_ref[:, ring.me] = wq_ref[...].reshape(3, HEAD, C)
-    ring.to_right(0).start()
-    ring.to_left(0).start()
-
-
-def ring_step(ring, s, inner=False):
-    ring.to_right(s - 1).wait_recv()
-    if inner or s < RIGHT_STEPS:
-        ring.to_right(s).start()
-    ring.left_to_core(s).start()
-    if inner or s <= LEFT_STEPS:
-        ring.to_left(s - 1).wait_recv()
-        if inner or s < LEFT_STEPS:
-            ring.to_left(s).start()
-        ring.right_to_core(s).start()
-
-
-def ring_end(ring):
-    for s in range(RIGHT_STEPS + 1):
-        if s >= 1:
-            ring.left_to_core(s).wait()
-        if 1 <= s <= LEFT_STEPS:
-            ring.right_to_core(s).wait()
-        if s < RIGHT_STEPS:
-            ring.to_right(s).wait_send()
-        if s < LEFT_STEPS:
-            ring.to_left(s).wait_send()
+            rows, rows, self.send.at[j], self.recv.at[head],
+            device_id={"slide": shift(self.me, j, SLIDES)}, device_id_type=MESH)
+
+    def along_y(self, j):
+        peer = (self.tile & ~6) | (((self.y + j) & 3) << 1)
+        rows = self.w3_ref.at[:, :, pl.ds(self.row, 16)]
+        return pltpu.make_async_remote_copy(
+            rows, rows, self.share.at[3 + j], self.share.at[jnp.minimum(self.y, 2)],
+            device_id={"tile": peer}, device_id_type=MESH)
+
+    def start(self, wq_ref):
+        @pl.when(self.source)
+        def _():
+            for part in range(3):
+                self.w3_ref[part, self.me >> 3, pl.ds(self.row, 16)] = wq_ref[
+                    pl.ds(pl.multiple_of(part * HEAD + self.row, 16), 16)]
+
+            @pl.loop(1, SLIDES)
+            def _(j):
+                self.along_z(j).start()
+
+    def hand_on(self):
+        @pl.when(self.carrier)
+        def _():
+            for head in range(SHARE):
+
+                @pl.when(self.me != self.member + MEMBERS * head)
+                def _():
+                    rows = self.w3_ref.at[:, head, pl.ds(0, 16)]
+                    pltpu.make_async_copy(rows, rows, self.recv.at[head]).wait()
+
+            for j in range(1, 4):
+                self.along_y(j).start()
+
+    def finish(self):
+        for y in range(3):
+
+            @pl.when(self.y != y)
+            def _():
+                rows = self.w3_ref.at[:, :, pl.ds(16 * y, 16)]
+                pltpu.make_async_copy(rows, rows, self.share.at[y]).wait()
+
+    def end(self):
+        @pl.when(self.source)
+        def _():
+            @pl.loop(1, SLIDES)
+            def _(j):
+                self.along_z(j).wait_send()
+
+        @pl.when(self.carrier)
+        def _():
+            for j in range(1, 4):
+                self.along_y(j).wait_send()
+
+
+def members_start(out_ref, in_ref, sems, n, same=False):
+    tile = lax.axis_index("tile")
+    member = (tile >> 3) * 2 + (tile & 1)
+    if not same:
+        in_ref[member] = out_ref[member]
+
+    @pl.loop(1, MEMBERS)
+    def _(j):
+        peer = shift(member, j, MEMBERS)
+        pltpu.make_async_remote_copy(
+            in_ref.at[member] if same else out_ref.at[peer], in_ref.at[member],
+            sems.at[0, n], sems.at[1, n],
+            device_id={"tile": (peer >> 1) * 8 + (tile & 6) + (peer & 1)}, device_id_type=MESH).start()
+
+
+def members_wait(in_ref, sems, n):
+    some = in_ref.at[pl.ds(0, MEMBERS - 1)]
+    pltpu.make_async_copy(some, some, sems.at[1, n]).wait()
+    pltpu.make_async_copy(some, some, sems.at[0, n]).wait()
 
 
 def exchange_start(out_ref, in_ref, send_sem, recv_sem):
@@ -409,32 +440,34 @@
     attn_ref, sums_ref,
     rows_ref, xt_ref, cv_ref, inv_ref, wb_ref, win_ref, w3_ref,
     out_ref, in_ref, back_out_ref, back_in_ref,
+    pick_ref, cot_out_ref, cot_in_ref, blocks_ref, part_out_ref, part_in_ref, mixed_out_ref, mixed_in_ref,
     part_ref, flat_ref, near_ref, far_ref, far_out_ref, res_ref,
-    local_sems, right_send, right_recv, left_send, left_recv, core_send, core_recv, route_sems, sum_sems,
+    local_sems, weight_send, weight_recv, share_sems, member_sems, route_sems, sum_sems,
 ):
     greet()
     for r in range(SIDE):
         map_copy(maps_ref, rows_ref, local_sems, r).start()
     win_copy = pltpu.make_async_copy(win_hbm, win_ref, local_sems.at[SIDE])
     win_copy.start()
-    ring = Ring(w3_ref, (right_send, right_recv, left_send, left_recv, core_send, core_recv))
-    w3_ref[:, ring.me] = wq_ref[...].reshape(3, HEAD, C)
+    weights = Weights(w3_ref, weight_send, weight_recv, share_sems)
+    member = weights.member
+    pick_ref[...] = member_columns()
+    cots = dot(cot_ref[...], pick_ref[...])
+    cut = jnp.full((ROWS, LANE), len_ref[0, 0], jnp.int32).astype(F32)
+    spare = iota((ROWS, LANE), 1) >= COLS
+    for m in range(MEMBERS):
+        cot_out_ref[m] = jnp.where(spare, cut, cots[:, m * LANE : (m + 1) * LANE]).astype(BF)
     spread_taps(dw_ref, wb_ref)
+    transpose_maps(maps_ref, rows_ref, local_sems, xt_ref)
     greeted()
-    ring.to_right(0).start()
-    ring.to_left(0).start()
-    transpose_maps(maps_ref, rows_ref, local_sems, xt_ref)
-
-    @pl.loop(0, 2)
-    def _(half):
-        @pl.loop(0, CHUNKS // 2)
-        def _(chunk):
-            conv_chunk(half * (CHUNKS // 2) + chunk, xt_ref, wb_ref, bias_ref, cv_ref)
-
-        ring_step(ring, half + 1, True)
+    weights.start(wq_ref)
+    members_start(cot_out_ref, cot_in_ref, member_sems, 0)
+
+    @pl.loop(0, CHUNKS)
+    def _(chunk):
+        conv_chunk(chunk, xt_ref, wb_ref, bias_ref, cv_ref)
 
     total = normalise(cv_ref, inv_ref, (0, SIDE), jnp.zeros((ROWS, C), F32))
-    ring_step(ring, 3)
     gain = gain_ref[...].reshape(1, C)
     pooled = (total * gain * (1.0 / AREA)).astype(BF)
     win_copy.wait()
@@ -444,18 +477,34 @@
     packed = jnp.concatenate([spread(embed), slots], axis=0)
     out_ref[...] = dot(select, packed).astype(BF).reshape(SLIDES, PACK, LANE)
     exchange_start(out_ref, in_ref, route_sems.at[0], route_sems.at[1])
+    weights.hand_on()
     spread_slots, mask = slot_spread(), head_mask()
-    allowed = allowed_pairs(seg_ref, dil_ref, len_ref)
-    for s in range(4, RIGHT_STEPS + 1):
-        ring_step(ring, s)
+    members_wait(cot_in_ref, member_sems, 0)
+    upstream = cot_in_ref[...].reshape(WIDE, LANE)
+    cut = upstream[:, COLS : COLS + 1].astype(F32).astype(jnp.int32)
+    allowed = allowed_pairs(member, seg_ref, dil_ref, cut)
     exchange_wait(out_ref, in_ref, route_sems.at[0], route_sems.at[1])
     arrived = in_ref[...].reshape(SLIDES * PACK, LANE)
     place = place_rows(spread_slots, arrived)
-    block = gather_chunks(dot_first(place, arrived).astype(BF))
-    ring_end(ring)
-    dblock = attention(block, w3_ref, cot_ref, attn_ref, mask, allowed)
+    blocks_ref[member] = gather_chunks(dot_first(place, arrived).astype(BF))
+    members_start(None, blocks_ref, member_sems, 1, True)
+    weights.finish()
+    members_wait(blocks_ref, member_sems, 1)
+    mixed, partial = attention(
+        blocks_ref[...].reshape(WIDE, C), upstream[:, :COLS], w3_ref, mask, allowed)
+    part_out_ref[...] = partial.astype(BF).reshape(MEMBERS, ROWS, C)
+    members_start(part_out_ref, part_in_ref, member_sems, 2)
+    padded = jnp.concatenate([mixed, jnp.zeros((WIDE, LANE - COLS), F32)], axis=1)
+    mixed_out_ref[...] = padded.astype(BF).reshape(MEMBERS, ROWS, LANE)
+    members_start(mixed_out_ref, mixed_in_ref, member_sems, 3)
+    members_wait(part_in_ref, member_sems, 2)
+    dblock = jnp.sum(part_in_ref[...].astype(F32), axis=0).astype(BF)
     back_out_ref[...] = dot(place, spread(dblock)).astype(BF).reshape(SLIDES, PACK, LANE)
     exchange_start(back_out_ref, back_in_ref, route_sems.at[2], route_sems.at[3])
+    members_wait(mixed_in_ref, member_sems, 3)
+    every = jnp.concatenate([mixed_in_ref[m] for m in range(MEMBERS)], axis=1)
+    attn_ref[...] = dot_last(every, pick_ref[...]).astype(BF)
+    weights.end()
     exchange_wait(back_out_ref, back_in_ref, route_sems.at[2], route_sems.at[3])
     returned = back_in_ref[...].reshape(SLIDES * PACK, LANE)
     dembed = gather_chunks(dot_first(select[:, : CHUNKS * ROWS], returned).astype(BF))
@@ -508,6 +557,8 @@
     dma = pltpu.SemaphoreType.DMA
     hbm = [pl.BlockSpec(memory_space=pl.ANY)]
     message = pltpu.VMEM((SLIDES, PACK, LANE), BF)
+    wide = pltpu.VMEM((MEMBERS, ROWS, C), BF)
+    narrow = pltpu.VMEM((MEMBERS, ROWS, LANE), BF)
     attn, sums = pl.pallas_call(
         step_kernel,
         out_shape=[shape(ROWS, C), shape(SUM_ROWS, C)],
@@ -517,12 +568,12 @@
             pltpu.VMEM((SIDE, ROWS, SIDE, C), BF), pltpu.VMEM((SIDE, SIDE, ROWS, C), F32),
             pltpu.VMEM((AREA, ROWS, C), F32), pltpu.VMEM((AREA, ROWS, LANE), F32),
             pltpu.VMEM((49, 8, C), F32), pltpu.VMEM((C, C), BF),
-            pltpu.VMEM((3, HEADS, HEAD, C), BF), message, message, message, message,
+            pltpu.VMEM((3, SHARE, HEAD, C), BF), message, message, message, message,
+            pltpu.VMEM((C, MEMBERS * LANE), BF), narrow, narrow, wide, wide, wide, narrow, narrow,
             pltpu.VMEM((SUM_ROWS, C), F32), pltpu.VMEM((SUM_ROWS, C), BF),
             pltpu.VMEM((PLANE, 16, LANE), BF), pltpu.VMEM((SLIDES, 16, LANE), BF),
             pltpu.VMEM((2, 16, LANE), BF), pltpu.VMEM((SUM_ROWS, C), BF),
-            dma((9,)), dma((9,)), dma((9,)), dma((9,)), dma((9,)), dma((2, 9)), dma((2, 9)), dma((4,)),
-            dma((6,)),
+            dma((9,)), dma((16,)), dma((2,)), dma((7,)), dma((2, 4)), dma((4,)), dma((6,)),
         ],
         compiler_params=params(collective_id=1, has_side_effects=True),
     )(

time: 106 us -> 96.6 us (0.911)
  Pallas kernels: 106 us -> 95.7 us
    pallas_call x1, Pallas kernels: 104 us -> 94.1 us  [body(): pl.pallas_call(step_kernel, out_shape=[shape(ROWS, C), shape(SUM_ROWS, C)...]
where the time goes in v3:
time: 96.6 us; the launch traced here: 96.4 us
  Pallas kernels  95.7 us (99%)
    pallas_call x1, Pallas kernels, body(): pl.pallas_call(step_kernel, out_shape=[shape(ROWS, C), shape(SUM_ROWS, C)...  94.1 us

profile of v3, /device:TPU:1, one launch (start us, length us, event | category | flops | bytes accessed | tf_op | source)
XLA Modules:
  0.0 96.4 jit_solution(15836256718129338228)
XLA Ops:
  0.6 94.1 %shard_map.130 = (bf16[16,768]{1,0:T(8,128)(2,1)}, bf16[64,768]{1,0:T(8,128)(2,1)}) custom-call(bf16[16,8,8,768]{3,2,1,0:T(8,128)(2,1)} %maps_ref.1, bf16[49,768]{1,0:T(8,128)(2,1)} %dw_ref.1, f32[768]{0:T(1024)} %bias_ref.1, f32[768]{0:T(1024)} %gain_ref.1, bf16[768,768]{1,0:T(8,128)(2,1)} %win_hbm.1, bf16[144,768]{1,0:T(8,128)(2,1)} %bitcast.1, ...), custom_call_target="tpu_custom_call" | custom-call | tf_op jit(solution)/shard_map/pallas_call | solution.py:562
  94.8 1.6 %shard_map.131 = (bf16[16,768]{1,0:T(8,128)(2,1)}, f32[49,768]{1,0:T(8,128)}, f32[2,768]{1,0:T(2,128)}) custom-call(bf16[16,768]{1,0:T(8,128)(2,1)} %get-tuple-element.5.attn_ref, bf16[64,768]{1,0:T(8,128)(2,1)} %get-tuple-element.6.res_ref), custom_call_target="tpu_custom_call" | custom-call | tf_op jit(solution)/shard_map/pallas_call | solution.py:583

commit v4 on v3

--- a/solution.py
+++ b/solution.py
@@ -74,30 +74,79 @@
         xt_ref[r] = dot(perm, part).reshape(SIDE, ROWS, C)
 
 
+POINTS = 20
+
+
+def points(a):
+    u = [a[0] + a[6], a[1] + a[7] if len(a) > 7 else a[1]] + a[2:6]
+    v = [a[0] - a[6], a[1] - a[7] if len(a) > 7 else a[1]] + a[2:6]
+    p = [u[k] + u[k + 3] for k in range(3)]
+    q = [u[k] - u[k + 3] for k in range(3)]
+    c0, c1 = p[0] - p[2], p[1] - p[2]
+    e0, e1 = q[0] - q[2], q[1] + q[2]
+    g0, g1 = v[0] - v[2] + v[4], v[1] - v[3] + v[5]
+    h0, h1, h2, h3 = v[0] - v[4], v[1] - v[5], v[2] + v[4], v[3] + v[5]
+    s0, s1 = h0 + h2, h1 + h3
+    return [
+        p[0] + p[1] + p[2], c0, c1, c0 + c1, q[0] - q[1] + q[2], e0, e1, e0 + e1,
+        g0, g1, g0 + g1, h0, h1, h0 + h1, h2, h3, h2 + h3, s0, s1, s0 + s1,
+    ]
+
+
+POINT_SCALE = [0.25] * 8 + [0.5] * 12
+
+
+def coefficients(m):
+    third = 1.0 / 3.0
+    c0, c1 = m[1] - m[2], m[3] - m[1] - m[2] - m[2]
+    p2 = (m[0] - c0 - c1) * third
+    p = [c0 + p2, c1 + p2, p2]
+    e0, e1 = m[5] - m[6], m[7] - m[5]
+    q2 = (m[4] - e0 + e1) * third
+    q = [e0 + q2, e1 - q2, q2]
+    u = [p[k] + q[k] for k in range(3)] + [p[k] - q[k] for k in range(3)]
+    g0, g1 = m[8] - m[9], m[10] - m[8] - m[9]
+    a1, b1, s1 = m[13] - m[11] - m[12], m[16] - m[14] - m[15], m[19] - m[17] - m[18]
+    s0, s2 = m[17] - m[11], m[18] - m[12]
+    h0 = m[11] - m[14] - s2
+    h1 = a1 - b1
+    h2 = m[12] - m[15] + s0 + s2
+    h3 = s1 - a1
+    v4, v5 = (g0 - h0 + h2) * third, (g1 - h1 + h3) * third
+    v = [h0 + v4, h1 + v5, h2 - v4, h3 - v5, v4, v5]
+    return [u[k] + v[k] for k in (3, 4, 5)] + [u[k] - v[k] for k in range(5)]
+
+
 def spread_taps(dw_ref, wb_ref):
     taps = dw_ref[...].astype(F32)
-    for tap in range(TAPS * TAPS):
-        wb_ref[tap] = jnp.broadcast_to(taps[tap : tap + 1], (8, C))
-
-
-def conv_chunk(chunk, xt_ref, wb_ref, bias_ref, cv_ref):
+    for r in range(TAPS):
+        row = [taps[r * TAPS + s : r * TAPS + s + 1] for s in range(TAPS)]
+        for f, point in enumerate(points(row[::-1])):
+            wb_ref[f, r] = jnp.broadcast_to(point * POINT_SCALE[f], (8, C))
+
+
+def conv_chunk(chunk, xt_ref, xp_ref, yp_ref, wb_ref, bias_ref, cv_ref):
     lanes = pl.ds(pl.multiple_of(chunk * LANE, LANE), LANE)
-    bias = jnp.broadcast_to(bias_ref[lanes].reshape(1, LANE), (2, 8, LANE))
+    bias = jnp.broadcast_to(bias_ref[lanes].reshape(1, LANE), (ROWS, LANE))
     for i in range(SIDE):
-        total = [bias] * SIDE
-        for r in range(TAPS):
-            src = i + r - REACH
-            if not 0 <= src < SIDE:
-                continue
-            cells = [xt_ref[src, j, :, lanes].reshape(2, 8, LANE) for j in range(SIDE)]
-            taps = [wb_ref[r * TAPS + s, :, lanes] for s in range(TAPS)]
-            for j in range(SIDE):
-                for s in range(TAPS):
-                    at = j + s - REACH
-                    if 0 <= at < SIDE:
-                        total[j] = total[j] + cells[at] * taps[s]
-        for j in range(SIDE):
-            cv_ref[i * SIDE + j, :, lanes] = total[j].reshape(ROWS, LANE)
+        for f, point in enumerate(points([xt_ref[i, j, :, lanes] for j in range(SIDE)])):
+            xp_ref[f, i, :, lanes] = point
+
+    @pl.loop(0, POINTS)
+    def _(f):
+        cells = [xp_ref[f, i, :, lanes].reshape(2, 8, LANE) for i in range(SIDE)]
+        taps = [wb_ref[f, r, :, lanes] for r in range(TAPS)]
+        for i in range(SIDE):
+            total = None
+            for r in range(TAPS):
+                if 0 <= i + r - REACH < SIDE:
+                    term = cells[i + r - REACH] * taps[r]
+                    total = term if total is None else total + term
+            yp_ref[f, i] = total.reshape(ROWS, LANE)
+
+    for i in range(SIDE):
+        for j, value in enumerate(coefficients([yp_ref[f, i] for f in range(POINTS)])):
+            cv_ref[i * SIDE + j, :, lanes] = value + bias
 
 
 def normalise(cv_ref, inv_ref, rows, total):
@@ -356,19 +405,25 @@
     return lax.fori_loop(0, SIDE, step, jnp.zeros((ROWS, C), F32))
 
 
-def tap_grads(chunk, xt_ref, cv_ref, part_ref):
+def tap_grads(chunk, xp_ref, yp_ref, cv_ref, sp_ref):
     lanes = pl.ds(pl.multiple_of(chunk * LANE, LANE), LANE)
-    for r in range(TAPS):
-        total = [jnp.zeros((ROWS, LANE), F32)] * TAPS
-        for i in range(*row_span(r - REACH)):
-            cells = [xt_ref[i + r - REACH, j, :, lanes] for j in range(SIDE)]
-            grads = [cv_ref[i * SIDE + j, :, lanes] for j in range(SIDE)]
-            for s in range(TAPS):
-                for j in range(*row_span(s - REACH)):
-                    total[s] = total[s] + cells[j + s - REACH] * grads[j]
-        for s in range(TAPS):
-            tap = r * TAPS + s
-            part_ref[tap : tap + 1, lanes] = jnp.sum(total[s], axis=0, keepdims=True)
+    for i in range(SIDE):
+        row = [cv_ref[i * SIDE + j, :, lanes] for j in range(SIDE)]
+        for f, point in enumerate(points(row[::-1])):
+            yp_ref[f, i] = point
+
+    @pl.loop(0, POINTS)
+    def _(f):
+        cells = [xp_ref[f, i, :, lanes] for i in range(SIDE)]
+        grads = [yp_ref[f, i] for i in range(SIDE)]
+        for r in range(TAPS):
+            total = None
+            for i in range(*row_span(r - REACH)):
+                term = cells[i + r - REACH] * grads[i]
+                total = term if total is None else total + term
+            sp_ref[f, r : r + 1] = jnp.sum(total, axis=0, keepdims=True)
+
+    return coefficients([sp_ref[f] * POINT_SCALE[f] for f in range(POINTS)])[1:]
 
 
 def unit_at(ref, unit):
@@ -381,20 +436,23 @@
     return unit + ((unit * 11) >> 5)
 
 
+def send_chunk(chunk, flat_ref, near_ref, sems):
+    tile = lax.axis_index("tile")
+    for rows in range(4):
+        unit = chunk * 4 + rows
+        peer = owner_of(unit)
+
+        @pl.when(peer != tile)
+        def _():
+            pltpu.make_async_remote_copy(
+                unit_at(flat_ref, unit), near_ref.at[tile], sems.at[0], sems.at[1],
+                device_id={"tile": peer}, device_id_type=MESH).start()
+
+
 def reduce_all(flat_ref, near_ref, far_ref, res_ref, far_out_ref, sems):
     tile, me = lax.axis_index("tile"), lax.axis_index("slide")
     owner = (tile & 3) != 3
     unit = jnp.minimum((tile >> 2) * 3 + (tile & 3), UNITS - 1)
-
-    @pl.loop(0, UNITS)
-    def _(j):
-        peer = owner_of(j)
-
-        @pl.when(peer != tile)
-        def _():
-            pltpu.make_async_remote_copy(
-                unit_at(flat_ref, j), near_ref.at[tile], sems.at[0], sems.at[1],
-                device_id={"tile": peer}, device_id_type=MESH).start()
 
     def wait_units(ref, count, sem):
         some = pl.ds(0, count)
@@ -441,7 +499,7 @@
     rows_ref, xt_ref, cv_ref, inv_ref, wb_ref, win_ref, w3_ref,
     out_ref, in_ref, back_out_ref, back_in_ref,
     pick_ref, cot_out_ref, cot_in_ref, blocks_ref, part_out_ref, part_in_ref, mixed_out_ref, mixed_in_ref,
-    part_ref, flat_ref, near_ref, far_ref, far_out_ref, res_ref,
+    xp_ref, yp_ref, sp_ref, norm_ref, flat_ref, near_ref, far_ref, far_out_ref, res_ref,
     local_sems, weight_send, weight_recv, share_sems, member_sems, route_sems, sum_sems,
 ):
     greet()
@@ -465,7 +523,7 @@
 
     @pl.loop(0, CHUNKS)
     def _(chunk):
-        conv_chunk(chunk, xt_ref, wb_ref, bias_ref, cv_ref)
+        conv_chunk(chunk, xt_ref, xp_ref, yp_ref, wb_ref, bias_ref, cv_ref)
 
     total = normalise(cv_ref, inv_ref, (0, SIDE), jnp.zeros((ROWS, C), F32))
     gain = gain_ref[...].reshape(1, C)
@@ -511,15 +569,21 @@
     dpool = dot_last(dembed, win_ref[...])
 
     bias_grad = conv_grads(dpool, gain, cv_ref, inv_ref)
-    part_ref[...] = jnp.zeros(part_ref.shape, F32)
-    part_ref[49:50] = jnp.sum(bias_grad, axis=0, keepdims=True)
-    part_ref[50:51] = jnp.sum(dpool * total, axis=0, keepdims=True) * (1.0 / AREA)
+    norm_ref[0:1] = jnp.sum(bias_grad, axis=0, keepdims=True)
+    norm_ref[1:2] = jnp.sum(dpool * total, axis=0, keepdims=True) * (1.0 / AREA)
+    sp_ref[...] = jnp.zeros(sp_ref.shape, F32)
 
     @pl.loop(0, CHUNKS)
     def _(chunk):
-        tap_grads(chunk, xt_ref, cv_ref, part_ref)
-
-    flat_ref[...] = part_ref[...].astype(BF)
+        lanes = pl.ds(pl.multiple_of(chunk * LANE, LANE), LANE)
+        blocks = tap_grads(chunk, xp_ref, yp_ref, cv_ref, sp_ref)
+        last = iota((8, LANE), 0) == TAPS
+        for k in range(2):
+            blocks[k] = jnp.where(last, norm_ref[k : k + 1, lanes], blocks[k])
+        blocks.append(jnp.zeros((8, LANE), F32))
+        flat_ref[:, lanes] = jnp.concatenate(blocks, axis=0).astype(BF)
+        send_chunk(chunk, flat_ref, near_ref, sum_sems)
+
     reduce_all(flat_ref, near_ref, far_ref, res_ref, far_out_ref, sum_sems)
     sums_ref[...] = res_ref[...]
 
@@ -527,8 +591,11 @@
 def finish_kernel(attn_ref, res_ref, out_ref, kernel_ref, norm_ref):
     out_ref[...] = attn_ref[...]
     result = res_ref[...].astype(F32)
-    kernel_ref[...] = result[:49]
-    norm_ref[...] = result[49:51]
+    for r in range(TAPS):
+        for s in range(TAPS):
+            kernel_ref[r * TAPS + s : r * TAPS + s + 1] = result[s * 8 + r : s * 8 + r + 1]
+    for k in range(2):
+        norm_ref[k : k + 1] = result[k * 8 + TAPS : k * 8 + TAPS + 1]
 
 
 VMEM_LIMIT = 60 * 1024 * 1024
@@ -567,10 +634,11 @@
         scratch_shapes=[
             pltpu.VMEM((SIDE, ROWS, SIDE, C), BF), pltpu.VMEM((SIDE, SIDE, ROWS, C), F32),
             pltpu.VMEM((AREA, ROWS, C), F32), pltpu.VMEM((AREA, ROWS, LANE), F32),
-            pltpu.VMEM((49, 8, C), F32), pltpu.VMEM((C, C), BF),
+            pltpu.VMEM((POINTS, TAPS, 8, C), F32), pltpu.VMEM((C, C), BF),
             pltpu.VMEM((3, SHARE, HEAD, C), BF), message, message, message, message,
             pltpu.VMEM((C, MEMBERS * LANE), BF), narrow, narrow, wide, wide, wide, narrow, narrow,
-            pltpu.VMEM((SUM_ROWS, C), F32), pltpu.VMEM((SUM_ROWS, C), BF),
+            pltpu.VMEM((POINTS, SIDE, ROWS, C), F32), pltpu.VMEM((POINTS, SIDE, ROWS, LANE), F32),
+            pltpu.VMEM((POINTS, 8, LANE), F32), pltpu.VMEM((2, C), F32), pltpu.VMEM((SUM_ROWS, C), BF),
             pltpu.VMEM((PLANE, 16, LANE), BF), pltpu.VMEM((SLIDES, 16, LANE), BF),
             pltpu.VMEM((2, 16, LANE), BF), pltpu.VMEM((SUM_ROWS, C), BF),
             dma((9,)), dma((16,)), dma((2,)), dma((7,)), dma((2, 4)), dma((4,)), dma((6,)),

time: 96.6 us -> 91.6 us (0.948)
  Pallas kernels: 95.7 us -> 90.8 us
    pallas_call x1, Pallas kernels: 94.1 us -> 89.2 us  [body(): pl.pallas_call(step_kernel, out_shape=[shape(ROWS, C), shape(SUM_ROWS, C)...]
where the time goes in v4:
time: 91.6 us; the launch traced here: 91.4 us
  Pallas kernels  90.8 us (99%)
    pallas_call x1, Pallas kernels, body(): pl.pallas_call(step_kernel, out_shape=[shape(ROWS, C), shape(SUM_ROWS, C)...  89.2 us

profile of v4, /device:TPU:1, one launch (start us, length us, event | category | flops | bytes accessed | tf_op | source)
XLA Modules:
  0.0 91.4 jit_solution(8198966969687326228)
XLA Ops:
  0.6 89.2 %shard_map.130 = (bf16[16,768]{1,0:T(8,128)(2,1)}, bf16[64,768]{1,0:T(8,128)(2,1)}) custom-call(bf16[16,8,8,768]{3,2,1,0:T(8,128)(2,1)} %maps_ref.1, bf16[49,768]{1,0:T(8,128)(2,1)} %dw_ref.1, f32[768]{0:T(1024)} %bias_ref.1, f32[768]{0:T(1024)} %gain_ref.1, bf16[768,768]{1,0:T(8,128)(2,1)} %win_hbm.1, bf16[144,768]{1,0:T(8,128)(2,1)} %bitcast.1, ...), custom_call_target="tpu_custom_call" | custom-call | tf_op jit(solution)/shard_map/pallas_call | solution.py:629
  89.8 1.6 %shard_map.131 = (bf16[16,768]{1,0:T(8,128)(2,1)}, f32[49,768]{1,0:T(8,128)}, f32[2,768]{1,0:T(2,128)}) custom-call(bf16[16,768]{1,0:T(8,128)(2,1)} %get-tuple-element.5.attn_ref, bf16[64,768]{1,0:T(8,128)(2,1)} %get-tuple-element.6.res_ref), custom_call_target="tpu_custom_call" | custom-call | tf_op jit(solution)/shard_map/pallas_call | solution.py:651

commit v5 on v4

--- a/solution.py
+++ b/solution.py
@@ -132,7 +132,7 @@
         for f, point in enumerate(points([xt_ref[i, j, :, lanes] for j in range(SIDE)])):
             xp_ref[f, i, :, lanes] = point
 
-    @pl.loop(0, POINTS)
+    @pl.loop(0, POINTS, unroll=5)
     def _(f):
         cells = [xp_ref[f, i, :, lanes].reshape(2, 8, LANE) for i in range(SIDE)]
         taps = [wb_ref[f, r, :, lanes] for r in range(TAPS)]
@@ -208,10 +208,14 @@
     return ((lane >= low) & (lane < low + HEAD)).astype(F32).astype(BF)
 
 
+def first_head(member):
+    return (member >> 1) + 4 * (member & 1)
+
+
 def member_columns():
     row, col = iota((C, MEMBERS * LANE), 0), iota((C, MEMBERS * LANE), 1)
     lane = col & (LANE - 1)
-    first = (col >> 7) * HEAD + lane
+    first = first_head(col >> 7) * HEAD + lane
     want = jnp.where(lane < HEAD, first, first + (MEMBERS - 1) * HEAD)
     want = jnp.where(lane < COLS, want, -1)
     return (row == want).astype(F32).astype(BF)
@@ -228,7 +232,8 @@
     apart = jnp.where((left >> 4) != (right >> 4), apart | 256, apart)
     parts = []
     for h in range(SHARE):
-        seg, dil = seg_ref[member + MEMBERS * h], dil_ref[member + MEMBERS * h]
+        head = first_head(member) + MEMBERS * h
+        seg, dil = seg_ref[head], dil_ref[head]
         parts.append(apart & (~(seg - 1) | (dil - 1)))
     return jnp.concatenate(parts, axis=0) == 0
 
@@ -264,22 +269,45 @@
     return (index + by + size) & (size - 1)
 
 
+def place_of(member, y):
+    return (member >> 1) * 8 + y * 2 + (member & 1)
+
+
 class Weights:
-    def __init__(self, w3_ref, send_sems, recv_sems, share_sems):
-        self.w3_ref, self.send, self.recv, self.share = w3_ref, send_sems, recv_sems, share_sems
+    def __init__(self, w3_ref, own_ref, send_sems, recv_sems, share_sems):
+        self.w3_ref, self.own_ref = w3_ref, own_ref
+        self.send, self.recv, self.share = send_sems, recv_sems, share_sems
         self.tile, self.me = lax.axis_index("tile"), lax.axis_index("slide")
         self.y = (self.tile >> 1) & 3
         self.member = (self.tile >> 3) * 2 + (self.tile & 1)
         self.carrier = self.y < 3
         self.row = pl.multiple_of(jnp.minimum(self.y, 2) * 16, 16)
-        self.source = self.carrier & ((self.me & 7) == self.member)
-
-    def along_z(self, j):
-        head = self.me >> 3
-        rows = self.w3_ref.at[:, head, pl.ds(self.row, 16)]
+        self.first = first_head(self.member)
+
+    def greet(self):
+        @pl.when(self.carrier)
+        def _():
+            for head in range(SHARE):
+                source = self.first + MEMBERS * head
+                j = shift(self.me, -source, SLIDES)
+
+                @pl.when(j != 0)
+                def _():
+                    pl.semaphore_signal(
+                        pltpu.get_barrier_semaphore(), inc=1,
+                        device_id={"tile": place_of(j & 7, self.y), "slide": source}, device_id_type=MESH)
+
+    def greetings(self):
+        return jnp.where(self.carrier, jnp.where(self.member == 0, 1, 2), 0)
+
+    def along_z(self, k):
+        low = self.me & 7
+        target = ((low & 3) << 1) | (low >> 2)
         return pltpu.make_async_remote_copy(
-            rows, rows, self.send.at[j], self.recv.at[head],
-            device_id={"slide": shift(self.me, j, SLIDES)}, device_id_type=MESH)
+            self.own_ref, self.w3_ref.at[:, self.me >> 3, pl.ds(self.row, 16)],
+            self.send.at[k], self.recv.at[self.me >> 3],
+            device_id={"tile": place_of(target, self.y), "slide": shift(self.me, self.member + 8 * k, SLIDES)},
+            device_id_type=MESH)
 
     def along_y(self, j):
         peer = (self.tile & ~6) | (((self.y + j) & 3) << 1)
@@ -289,22 +317,27 @@
             device_id={"tile": peer}, device_id_type=MESH)
 
     def start(self, wq_ref):
-        @pl.when(self.source)
+        @pl.when(self.carrier)
         def _():
             for part in range(3):
-                self.w3_ref[part, self.me >> 3, pl.ds(self.row, 16)] = wq_ref[
-                    pl.ds(pl.multiple_of(part * HEAD + self.row, 16), 16)]
-
-            @pl.loop(1, SLIDES)
-            def _(j):
-                self.along_z(j).start()
+                self.own_ref[part] = wq_ref[pl.ds(pl.multiple_of(part * HEAD + self.row, 16), 16)]
+
+            self.along_z(1).start()
+
+            @pl.when(self.member != 0)
+            def _():
+                self.along_z(0).start()
+
+            @pl.when((self.me & 7) == self.first)
+            def _():
+                self.w3_ref[:, self.me >> 3, pl.ds(self.row, 16)] = self.own_ref[...]
 
     def hand_on(self):
         @pl.when(self.carrier)
         def _():
             for head in range(SHARE):
 
-                @pl.when(self.me != self.member + MEMBERS * head)
+                @pl.when(self.me != self.first + MEMBERS * head)
                 def _():
                     rows = self.w3_ref.at[:, head, pl.ds(0, 16)]
                     pltpu.make_async_copy(rows, rows, self.recv.at[head]).wait()
@@ -321,14 +354,14 @@
                 pltpu.make_async_copy(rows, rows, self.share.at[y]).wait()
 
     def end(self):
-        @pl.when(self.source)
-        def _():
-            @pl.loop(1, SLIDES)
-            def _(j):
-                self.along_z(j).wait_send()
-
         @pl.when(self.carrier)
         def _():
+            self.along_z(1).wait_send()
+
+            @pl.when(self.member != 0)
+            def _():
+                self.along_z(0).wait_send()
+
             for j in range(1, 4):
                 self.along_y(j).wait_send()
 
@@ -387,8 +420,8 @@
             barrier, inc=1, device_id={"tile": shift(tile, j, PLANE)}, device_id_type=MESH)
 
 
-def greeted():
-    pl.semaphore_wait(pltpu.get_barrier_semaphore(), SLIDES + PLANE - 2)
+def greeted(more):
+    pl.semaphore_wait(pltpu.get_barrier_semaphore(), SLIDES + PLANE - 2 + more)
 
 
 def conv_grads(dpool, gain, cv_ref, inv_ref):
@@ -412,7 +445,7 @@
         for f, point in enumerate(points(row[::-1])):
             yp_ref[f, i] = point
 
-    @pl.loop(0, POINTS)
+    @pl.loop(0, POINTS, unroll=5)
     def _(f):
         cells = [xp_ref[f, i, :, lanes] for i in range(SIDE)]
         grads = [yp_ref[f, i] for i in range(SIDE)]
@@ -496,18 +529,19 @@
 def step_kernel(
     maps_ref, dw_ref, bias_ref, gain_ref, win_hbm, wq_ref, seg_ref, dil_ref, slot_ref, len_ref, cot_ref,
     attn_ref, sums_ref,
-    rows_ref, xt_ref, cv_ref, inv_ref, wb_ref, win_ref, w3_ref,
+    rows_ref, xt_ref, cv_ref, inv_ref, wb_ref, win_ref, w3_ref, own_ref,
     out_ref, in_ref, back_out_ref, back_in_ref,
     pick_ref, cot_out_ref, cot_in_ref, blocks_ref, part_out_ref, part_in_ref, mixed_out_ref, mixed_in_ref,
     xp_ref, yp_ref, sp_ref, norm_ref, flat_ref, near_ref, far_ref, far_out_ref, res_ref,
     local_sems, weight_send, weight_recv, share_sems, member_sems, route_sems, sum_sems,
 ):
     greet()
+    weights = Weights(w3_ref, own_ref, weight_send, weight_recv, share_sems)
+    weights.greet()
     for r in range(SIDE):
         map_copy(maps_ref, rows_ref, local_sems, r).start()
     win_copy = pltpu.make_async_copy(win_hbm, win_ref, local_sems.at[SIDE])
     win_copy.start()
-    weights = Weights(w3_ref, weight_send, weight_recv, share_sems)
     member = weights.member
     pick_ref[...] = member_columns()
     cots = dot(cot_ref[...], pick_ref[...])
@@ -517,7 +551,7 @@
         cot_out_ref[m] = jnp.where(spare, cut, cots[:, m * LANE : (m + 1) * LANE]).astype(BF)
     spread_taps(dw_ref, wb_ref)
     transpose_maps(maps_ref, rows_ref, local_sems, xt_ref)
-    greeted()
+    greeted(weights.greetings())
     weights.start(wq_ref)
     members_start(cot_out_ref, cot_in_ref, member_sems, 0)
 
@@ -635,13 +669,13 @@
             pltpu.VMEM((SIDE, ROWS, SIDE, C), BF), pltpu.VMEM((SIDE, SIDE, ROWS, C), F32),
             pltpu.VMEM((AREA, ROWS, C), F32), pltpu.VMEM((AREA, ROWS, LANE), F32),
             pltpu.VMEM((POINTS, TAPS, 8, C), F32), pltpu.VMEM((C, C), BF),
-            pltpu.VMEM((3, SHARE, HEAD, C), BF), message, message, message, message,
+            pltpu.VMEM((3, SHARE, HEAD, C), BF), pltpu.VMEM((3, 16, C), BF), message, message, message, message,
             pltpu.VMEM((C, MEMBERS * LANE), BF), narrow, narrow, wide, wide, wide, narrow, narrow,
             pltpu.VMEM((POINTS, SIDE, ROWS, C), F32), pltpu.VMEM((POINTS, SIDE, ROWS, LANE), F32),
             pltpu.VMEM((POINTS, 8, LANE), F32), pltpu.VMEM((2, C), F32), pltpu.VMEM((SUM_ROWS, C), BF),
             pltpu.VMEM((PLANE, 16, LANE), BF), pltpu.VMEM((SLIDES, 16, LANE), BF),
             pltpu.VMEM((2, 16, LANE), BF), pltpu.VMEM((SUM_ROWS, C), BF),
-            dma((9,)), dma((16,)), dma((2,)), dma((7,)), dma((2, 4)), dma((4,)), dma((6,)),
+            dma((9,)), dma((2,)), dma((2,)), dma((7,)), dma((2, 4)), dma((4,)), dma((6,)),
         ],
         compiler_params=params(collective_id=1, has_side_effects=True),
     )(

time: 91.6 us -> 85.8 us (0.937)
  Pallas kernels: 90.8 us -> 85 us
    pallas_call x1, Pallas kernels: 89.2 us -> 83.4 us  [body(): pl.pallas_call(step_kernel, out_shape=[shape(ROWS, C), shape(SUM_ROWS, C)...]
where the time goes in v5:
time: 85.8 us; the launch traced here: 85.6 us
  Pallas kernels  85 us (99%)
    pallas_call x1, Pallas kernels, body(): pl.pallas_call(step_kernel, out_shape=[shape(ROWS, C), shape(SUM_ROWS, C)...  83.4 us

profile of v5, /device:TPU:1, one launch (start us, length us, event | category | flops | bytes accessed | tf_op | source)
XLA Modules:
  0.0 85.6 jit_solution(8818276263179964065)
XLA Ops:
  0.6 83.4 %shard_map.130 = (bf16[16,768]{1,0:T(8,128)(2,1)}, bf16[64,768]{1,0:T(8,128)(2,1)}) custom-call(bf16[16,8,8,768]{3,2,1,0:T(8,128)(2,1)} %maps_ref.1, bf16[49,768]{1,0:T(8,128)(2,1)} %dw_ref.1, f32[768]{0:T(1024)} %bias_ref.1, f32[768]{0:T(1024)} %gain_ref.1, bf16[768,768]{1,0:T(8,128)(2,1)} %win_hbm.1, bf16[144,768]{1,0:T(8,128)(2,1)} %bitcast.1, ...), custom_call_target="tpu_custom_call" | custom-call | tf_op jit(solution)/shard_map/pallas_call | solution.py:663
  84.0 1.6 %shard_map.131 = (bf16[16,768]{1,0:T(8,128)(2,1)}, f32[49,768]{1,0:T(8,128)}, f32[2,768]{1,0:T(2,128)}) custom-call(bf16[16,768]{1,0:T(8,128)(2,1)} %get-tuple-element.5.attn_ref, bf16[64,768]{1,0:T(8,128)(2,1)} %get-tuple-element.6.res_ref), custom_call_target="tpu_custom_call" | custom-call | tf_op jit(solution)/shard_map/pallas_call | solution.py:685

commit v6 on v5

--- a/solution.py
+++ b/solution.py
@@ -132,7 +132,7 @@
         for f, point in enumerate(points([xt_ref[i, j, :, lanes] for j in range(SIDE)])):
             xp_ref[f, i, :, lanes] = point
 
-    @pl.loop(0, POINTS, unroll=5)
+    @pl.loop(0, POINTS, unroll=10)
     def _(f):
         cells = [xp_ref[f, i, :, lanes].reshape(2, 8, LANE) for i in range(SIDE)]
         taps = [wb_ref[f, r, :, lanes] for r in range(TAPS)]
@@ -445,7 +445,7 @@
         for f, point in enumerate(points(row[::-1])):
             yp_ref[f, i] = point
 
-    @pl.loop(0, POINTS, unroll=5)
+    @pl.loop(0, POINTS, unroll=10)
     def _(f):
         cells = [xp_ref[f, i, :, lanes] for i in range(SIDE)]
         grads = [yp_ref[f, i] for i in range(SIDE)]
@@ -495,7 +495,6 @@
     def _():
         near_ref[tile] = unit_at(flat_ref, unit)[...]
         wait_units(near_ref, PLANE - 1, sems.at[1])
-        wait_units(near_ref, UNITS - 1, sems.at[0])
         near = jnp.sum(near_ref[...].astype(F32), axis=0).astype(BF)
         far_out_ref[0] = near
         far_ref[me] = near
@@ -516,6 +515,7 @@
                 far_out_ref.at[1], unit_at(res_ref, unit), sems.at[4], sems.at[5],
                 device_id={"tile": shift(tile, j, PLANE)}, device_id_type=MESH).start()
 
+        wait_units(near_ref, UNITS - 1, sems.at[0])
         wait_units(far_ref, SLIDES - 1, sems.at[2])
         wait_units(near_ref, PLANE - 1, sems.at[4])
 

time: 85.8 us -> 85.6 us (level)
  no operation moved by 1% of the time
where the time goes in v6:
time: 85.6 us; the launch traced here: 85.4 us
  Pallas kernels  84.8 us (99%)
    pallas_call x1, Pallas kernels, body(): pl.pallas_call(step_kernel, out_shape=[shape(ROWS, C), shape(SUM_ROWS, C)...  83.2 us

profile of v6, /device:TPU:1, one launch (start us, length us, event | category | flops | bytes accessed | tf_op | source)
XLA Modules:
  0.0 85.4 jit_solution(11488415240685502800)
XLA Ops:
  0.6 83.2 %shard_map.130 = (bf16[16,768]{1,0:T(8,128)(2,1)}, bf16[64,768]{1,0:T(8,128)(2,1)}) custom-call(bf16[16,8,8,768]{3,2,1,0:T(8,128)(2,1)} %maps_ref.1, bf16[49,768]{1,0:T(8,128)(2,1)} %dw_ref.1, f32[768]{0:T(1024)} %bias_ref.1, f32[768]{0:T(1024)} %gain_ref.1, bf16[768,768]{1,0:T(8,128)(2,1)} %win_hbm.1, bf16[144,768]{1,0:T(8,128)(2,1)} %bitcast.1, ...), custom_call_target="tpu_custom_call" | custom-call | tf_op jit(solution)/shard_map/pallas_call | solution.py:663
  83.8 1.6 %shard_map.131 = (bf16[16,768]{1,0:T(8,128)(2,1)}, f32[49,768]{1,0:T(8,128)}, f32[2,768]{1,0:T(2,128)}) custom-call(bf16[16,768]{1,0:T(8,128)(2,1)} %get-tuple-element.5.attn_ref, bf16[64,768]{1,0:T(8,128)(2,1)} %get-tuple-element.6.res_ref), custom_call_target="tpu_custom_call" | custom-call | tf_op jit(solution)/shard_map/pallas_call | solution.py:685
